TPU v7x, 32 devices: a whole 2x2x4 slice. The times are simulated.
32 devices in a mesh: lon: 4 (over x, core), lat: 4 (over z), tm: 2 (over y).
Axes of the slice: x: 2, y: 2, z: 4, core: 2. Of those that a mesh axis runs over, the one named last changes fastest.
Arguments:
- snapshots: float32 [16, 8, 64, 512], P('tm', None, 'lat', 'lon'), may hold values from -6 to 6
- basis: float32 [64, 8, 64, 512], P(None, None, 'lat', 'lon'), may hold values from -6 to 6
Outputs:
- new_basis: float32 [64, 8, 64, 512], P(None, None, 'lat', 'lon')
- coeffs: float32 [64, 16], P(None, 'tm')
All inputs are finite; a program needn't handle non-finite values.
Results may differ from a plain program's by a relative error of at most 0.00011.
Values sent between devices are 32-bit elements; how exact they have to be, the bound alone decides.
A program may use at most 64 MiB of HBM per device.

v0:
```python
import math

import jax
import jax.numpy as jnp
from jax import lax
from jax.sharding import PartitionSpec as P

SMOOTH_RATE = 0.1
STEP_SIZE = 0.25


def with_halo(cells, sides, width, closed):
    for axis, dim in sides:
        count = lax.axis_size(axis)
        ends = count if closed else count - 1
        head = lax.slice_in_dim(cells, 0, width, axis=dim)
        tail = lax.slice_in_dim(cells, cells.shape[dim] - width, cells.shape[dim], axis=dim)
        cells = jnp.concatenate(
            [
                lax.ppermute(tail, axis, [(i, (i + 1) % count) for i in range(ends)]),
                cells,
                lax.ppermute(head, axis, [((i + 1) % count, i) for i in range(ends)]),
            ],
            axis=dim,
        )
    return cells


def product(left, right):
    return jnp.dot(left, right, precision=lax.Precision.HIGHEST, preferred_element_type=jnp.float32)


def laplace_step(extended):
    padded = jnp.pad(extended, ((0, 0), (1, 1), (0, 0), (0, 0)))
    center = extended[:, :, 1:-1, 1:-1]
    neighbours = padded[:, 2:, 1:-1, 1:-1] + padded[:, :-2, 1:-1, 1:-1]
    neighbours = neighbours + extended[:, :, 2:, 1:-1] + extended[:, :, :-2, 1:-1]
    neighbours = neighbours + extended[:, :, 1:-1, 2:] + extended[:, :, 1:-1, :-2]
    return center + SMOOTH_RATE * (neighbours - 6.0 * center)


def finish(grown, gram_matrix):
    factor = jnp.linalg.cholesky(gram_matrix)
    return jax.scipy.linalg.solve_triangular(factor, grown, lower=True)


def shards(snapshots, basis):
    snap_count, levels, rows_lat, cols_lon = snapshots.shape
    eof_count = basis.shape[0]
    total_cells = levels * rows_lat * cols_lon * lax.axis_size("lat") * lax.axis_size("lon")
    inv_root = 1.0 / math.sqrt(total_cells)
    smoothed = snapshots
    for sweep in range(3):
        lat_wide = with_halo(smoothed, (("lat", 2),), 1, False)
        extended = with_halo(lat_wide, (("lon", 3),), 1, True)
        smoothed = laplace_step(extended)
    columns = basis.reshape(eof_count, -1)
    gathered = lax.all_gather(smoothed, "tm", axis=0, tiled=True)
    all_flat = gathered.reshape(gathered.shape[0], -1)
    coeffs_all = lax.psum(product(columns, all_flat.T), ("lon", "lat")) * inv_root
    grown = columns + STEP_SIZE * product(coeffs_all, all_flat)
    gram_matrix = lax.psum(product(grown, grown.T), ("lon", "lat")) / total_cells
    new_basis = finish(grown, gram_matrix)
    coeffs = lax.dynamic_slice_in_dim(coeffs_all, lax.axis_index("tm") * snap_count, snap_count, 1)
    return (new_basis.reshape(basis.shape), coeffs)


def solution(mesh):
    placed = (P("tm", None, "lat", "lon"), P(None, None, "lat", "lon"))
    return jax.shard_map(
        shards,
        mesh=mesh,
        in_specs=placed,
        out_specs=(P(None, None, "lat", "lon"), P(None, "tm")),
        check_vma=False,
    )
```

profile of v0, /device:TPU:0, one launch (start us, length us, event | category | flops | bytes accessed | tf_op | source)
XLA Modules:
  0.0 225.4 jit_solution(3377713470709653232)
XLA Ops:
  7.2 1.4 copy.43
  8.6 4.9 %collective-permute-start = (f32[8,8,1,128]{3,0,2,1:T(8,128)S(1)}, f32[8,8,1,128]{3,0,2,1:T(8,128)S(1)}, u32[]{:S(2)}, u32[]{:S(2)}) collective-permute-start(f32[8,8,1,128]{3,0,2,1:T(8,128)S(1)} %get-tuple-element.19), channel_id=1, source_target_pairs={{0,2},{2,4},{4,6},{1,3},{3,5},{5,7},{8,10},{10,12},{12,14},{9,11},... | collective-permute-start | bytes 98312 | tf_op jit(solution)/shard_map/ppermute | solution.py:20
  13.6 1.3 collective-permute-start.1
  15.5 3.9 %collective-permute-done.1 = f32[8,8,1,128]{3,0,2,1:T(8,128)S(1)} collective-permute-done((f32[8,8,1,128]{3,0,2,1:T(8,128)S(1)}, f32[8,8,1,128]{3,0,2,1:T(8,128)S(1)}, u32[]{:S(2)}, u32[]{:S(2)}) %collective-permute-start.1) | collective-permute-done | bytes 32800 | tf_op jit(solution)/shard_map/ppermute | solution.py:22
  19.6 0.5 copy.35
  20.6 0.5 collective-permute-start.2
  21.1 0.6 collective-permute-done.3
  21.7 0.5 copy.37
  22.2 1.8 collective-permute-done.2
  24.0 0.5 copy.36
  24.5 0.5 select_maximum_fusion.8
  25.0 0.8 fusion.28
  25.8 3.5 %collective-permute-start.4 = (f32[8,8,1,128]{3,0,2,1:T(8,128)S(1)}, f32[8,8,1,128]{3,0,2,1:T(8,128)S(1)}, u32[]{:S(2)}, u32[]{:S(2)}) collective-permute-start(f32[8,8,1,128]{3,0,2,1:T(8,128)S(1)} %get-tuple-element.16), channel_id=1, source_target_pairs={{0,2},{2,4},{4,6},{1,3},{3,5},{5,7},{8,10},{10,12},{12,14},{9,11},... | collective-permute-start | bytes 98312 | tf_op jit(solution)/shard_map/ppermute | solution.py:20
  29.3 1.3 collective-permute-start.5
  30.9 4.2 %collective-permute-done.5 = f32[8,8,1,128]{3,0,2,1:T(8,128)S(1)} collective-permute-done((f32[8,8,1,128]{3,0,2,1:T(8,128)S(1)}, f32[8,8,1,128]{3,0,2,1:T(8,128)S(1)}, u32[]{:S(2)}, u32[]{:S(2)}) %collective-permute-start.5) | collective-permute-done | bytes 32800 | tf_op jit(solution)/shard_map/ppermute | solution.py:22
  35.4 0.5 copy.45
  36.4 0.5 collective-permute-start.6
  36.9 0.6 collective-permute-done.7
  37.5 0.5 copy.47
  38.0 1.8 collective-permute-done.6
  39.7 0.5 copy.46
  40.2 0.5 select_maximum_fusion.4
  40.8 0.8 fusion.21
  41.6 3.5 %collective-permute-start.8 = (f32[8,8,1,128]{3,0,2,1:T(8,128)S(1)}, f32[8,8,1,128]{3,0,2,1:T(8,128)S(1)}, u32[]{:S(2)}, u32[]{:S(2)}) collective-permute-start(f32[8,8,1,128]{3,0,2,1:T(8,128)S(1)} %get-tuple-element.14), channel_id=1, source_target_pairs={{0,2},{2,4},{4,6},{1,3},{3,5},{5,7},{8,10},{10,12},{12,14},{9,11},... | collective-permute-start | bytes 98312 | tf_op jit(solution)/shard_map/ppermute | solution.py:20
  45.1 1.3 collective-permute-start.9
  46.6 4.2 %collective-permute-done.9 = f32[8,8,1,128]{3,0,2,1:T(8,128)S(1)} collective-permute-done((f32[8,8,1,128]{3,0,2,1:T(8,128)S(1)}, f32[8,8,1,128]{3,0,2,1:T(8,128)S(1)}, u32[]{:S(2)}, u32[]{:S(2)}) %collective-permute-start.9) | collective-permute-done | bytes 32800 | tf_op jit(solution)/shard_map/ppermute | solution.py:22
  51.1 0.5 copy.51
  52.2 0.7 collective-permute-start.10
  53.3 0.5 copy.53
  53.8 1.9 collective-permute-done.10
  55.7 0.5 copy.52
  56.2 0.5 select_maximum_fusion
  56.7 1.6 fusion.14
  58.3 19.6 %all-gather.2.cloned.1.call-done = f32[16,8,16,128]{3,0,2,1:T(8,128)} async-done(((f32[8,8,16,128]{3,0,2,1:T(8,128)}), f32[16,8,16,128]{3,0,2,1:T(8,128)}) %all-gather.2.cloned.1.call-update) | async-done | bytes 1048592 | tf_op jit(solution)/shard_map/all_gather | solution.py:58
  78.0 7.6 %fusion.6 = f32[64,16]{0,1:T(8,128)S(1)} fusion(f32[16,8,16,128]{3,0,2,1:T(8,128)} %all-gather.2.cloned.1.call-done, f32[64,8,16,128]{3,2,1,0:T(8,128)} %param.3), kind=kOutput, calls=%fused_computation.19 | convolution fusion | flops 201326592 | bytes 5246976 | tf_op jit(solution)/shard_map/dot_general | solution.py:30
  85.5 34.2 %psum.14 = f32[64,16]{0,1:T(8,128)S(1)} all-reduce(f32[64,16]{0,1:T(8,128)S(1)} %fusion.6), channel_id=1, replica_groups=mesh['lon'=4,'lat'=4,'tm'=2] {'lon','lat'}, use_global_device_ids=true, to_apply=%region_0.1 | all-reduce | flops 1024 | bytes 8192 | tf_op jit(solution)/shard_map/psum | solution.py:60
  120.2 8.6 %fusion = f32[64,16384]{1,0:T(8,128)S(1)} fusion(f32[8,8,128,128]{3,2,1,0:T(8,128)} %bitcast.36, f32[2,8,128,128]{3,2,1,0:T(8,128)S(1)} %bitcast.38, f32[64,16]{0,1:T(8,128)S(1)} %psum.14), kind=kOutput, calls=%fused_computation.1 | convolution fusion | flops 203424768 | bytes 9441280 | tf_op jit(solution)/shard_map/dot_general | solution.py:30
  128.8 2.0 copy-done
  130.8 3.4 %fusion.41 = f32[64,64]{0,1:T(8,128)S(1)} fusion(f32[64,16384]{1,0:T(8,128)S(1)} %fusion), kind=kOutput, calls=%fused_computation.89 | convolution fusion | flops 805306368 | bytes 4210688 | tf_op jit(solution)/shard_map/dot_general | solution.py:30
  134.2 58.2 %psum.15 = f32[64,64]{0,1:T(8,128)S(1)} all-reduce(f32[64,64]{0,1:T(8,128)S(1)} %fusion.41), channel_id=1, replica_groups=mesh['lon'=4,'lat'=4,'tm'=2] {'lon','lat'}, use_global_device_ids=true, to_apply=%region_1.2 | all-reduce | flops 4096 | bytes 32768 | tf_op jit(solution)/shard_map/psum | solution.py:62
  192.5 5.8 %cholesky.16 = f32[64,64]{1,0:T(8,128)S(1)} custom-call(f32[64,64]{1,0:T(8,128)S(1)} %fusion.34), custom_call_target="Cholesky" | custom-call | tf_op jit(solution)/shard_map/jit(cholesky)/cholesky | solution.py:43
  198.4 0.6 compare_reduce_fusion
  199.0 0.7 fusion.32
  199.7 4.9 %custom-call.7 = f32[1,64,64]{1,2,0:T(8,128)S(1)} custom-call(f32[1,64,64]{2,1,0:T(8,128)S(1)} %fusion.32), custom_call_target="InvertDiagBlocksLowerTriangular" | custom-call | tf_op jit(solution)/shard_map/jit(_solve_triangular)/triangular_solve | solution.py:44
  204.6 2.9 %copy.69 = f32[8,8,128,128]{3,2,1,0:T(8,128)S(1)} copy(f32[8,8,128,128]{3,1,2,0:T(8,128)} %bitcast.35) | data formatting | bytes 8388608
  207.5 6.0 %fusion.1 = f32[64,8,16,128]{3,0,2,1:T(8,128)S(1)} fusion(f32[8,16,128,64]{2,1,0,3:T(8,128)S(1)} %bitcast.37, f32[1,64,64]{1,2,0:T(8,128)S(1)} %custom-call.7), kind=kOutput, calls=%fused_computation.2 | convolution fusion | flops 805306368 | bytes 8404992 | tf_op jit(solution)/shard_map/jit(_solve_triangular)/triangular_solve | solution.py:44
  213.5 4.4 %copy.62 = f32[64,8,16,128]{3,2,1,0:T(8,128)} copy(f32[64,8,16,128]{3,0,2,1:T(8,128)S(1)} %fusion.1) | data formatting | bytes 8388608
  217.9 0.6 constant_dynamic-slice_fusion
  (34 shorter events, 4.4 us)
Async XLA Ops:
  7.2 8.0 %copy-start.2 = (f32[8,8,16,128]{3,2,1,0:T(8,128)S(1)}, f32[8,8,16,128]{3,2,1,0:T(8,128)}, u32[]{:S(2)}) copy-start(f32[8,8,16,128]{3,2,1,0:T(8,128)} %param.2) | copy-start | bytes 1572868
  7.2 70.8 %all-gather.2.cloned.1.call-start = ((), (), s32[]{:S(2)}) async-start(), calls=%async_computation | async-start | bytes 1572864 | tf_op jit(solution)/shard_map/all_gather | solution.py:58
  8.6 6.5 %collective-permute-start = (f32[8,8,1,128]{3,0,2,1:T(8,128)S(1)}, f32[8,8,1,128]{3,0,2,1:T(8,128)S(1)}, u32[]{:S(2)}, u32[]{:S(2)}) collective-permute-start(f32[8,8,1,128]{3,0,2,1:T(8,128)S(1)} %get-tuple-element.19), channel_id=1, source_target_pairs={{0,2},{2,4},{4,6},{1,3},{3,5},{5,7},{8,10},{10,12},{12,14},{9,11},... | collective-permute-start | bytes 98312 | tf_op jit(solution)/shard_map/ppermute | solution.py:20
  13.6 5.8 %collective-permute-start.1 = (f32[8,8,1,128]{3,0,2,1:T(8,128)S(1)}, f32[8,8,1,128]{3,0,2,1:T(8,128)S(1)}, u32[]{:S(2)}, u32[]{:S(2)}) collective-permute-start(f32[8,8,1,128]{3,0,2,1:T(8,128)S(1)} %get-tuple-element.18), channel_id=1, source_target_pairs={{2,0},{4,2},{6,4},{3,1},{5,3},{7,5},{10,8},{12,10},{14,12},{11,9},... | collective-permute-start | bytes 98312 | tf_op jit(solution)/shard_map/ppermute | solution.py:22
  20.1 1.6 collective-permute-start.3
  20.6 3.4 %collective-permute-start.2 = (f32[8,8,18,1]{2,1,3,0:T(8,128)S(1)}, f32[8,8,18,1]{2,1,3,0:T(8,128)S(1)}, u32[]{:S(2)}, u32[]{:S(2)}) collective-permute-start(f32[8,8,18,1]{2,1,3,0:T(8,128)S(1)} %copy.34), channel_id=1, source_target_pairs={{0,8},{8,16},{16,24},{24,0},{1,9},{9,17},{17,25},{25,1},{2,10},{10... | collective-permute-start | bytes 13832 | tf_op jit(solution)/shard_map/ppermute | solution.py:20
  25.8 5.1 %collective-permute-start.4 = (f32[8,8,1,128]{3,0,2,1:T(8,128)S(1)}, f32[8,8,1,128]{3,0,2,1:T(8,128)S(1)}, u32[]{:S(2)}, u32[]{:S(2)}) collective-permute-start(f32[8,8,1,128]{3,0,2,1:T(8,128)S(1)} %get-tuple-element.16), channel_id=1, source_target_pairs={{0,2},{2,4},{4,6},{1,3},{3,5},{5,7},{8,10},{10,12},{12,14},{9,11},... | collective-permute-start | bytes 98312 | tf_op jit(solution)/shard_map/ppermute | solution.py:20
  29.3 5.8 %collective-permute-start.5 = (f32[8,8,1,128]{3,0,2,1:T(8,128)S(1)}, f32[8,8,1,128]{3,0,2,1:T(8,128)S(1)}, u32[]{:S(2)}, u32[]{:S(2)}) collective-permute-start(f32[8,8,1,128]{3,0,2,1:T(8,128)S(1)} %get-tuple-element.17), channel_id=1, source_target_pairs={{2,0},{4,2},{6,4},{3,1},{5,3},{7,5},{10,8},{12,10},{14,12},{11,9},... | collective-permute-start | bytes 98312 | tf_op jit(solution)/shard_map/ppermute | solution.py:22
  35.9 1.6 collective-permute-start.7
  36.4 3.4 %collective-permute-start.6 = (f32[8,8,18,1]{2,1,3,0:T(8,128)S(1)}, f32[8,8,18,1]{2,1,3,0:T(8,128)S(1)}, u32[]{:S(2)}, u32[]{:S(2)}) collective-permute-start(f32[8,8,18,1]{2,1,3,0:T(8,128)S(1)} %copy.44), channel_id=1, source_target_pairs={{0,8},{8,16},{16,24},{24,0},{1,9},{9,17},{17,25},{25,1},{2,10},{10... | collective-permute-start | bytes 13832 | tf_op jit(solution)/shard_map/ppermute | solution.py:20
  41.6 5.1 %collective-permute-start.8 = (f32[8,8,1,128]{3,0,2,1:T(8,128)S(1)}, f32[8,8,1,128]{3,0,2,1:T(8,128)S(1)}, u32[]{:S(2)}, u32[]{:S(2)}) collective-permute-start(f32[8,8,1,128]{3,0,2,1:T(8,128)S(1)} %get-tuple-element.14), channel_id=1, source_target_pairs={{0,2},{2,4},{4,6},{1,3},{3,5},{5,7},{8,10},{10,12},{12,14},{9,11},... | collective-permute-start | bytes 98312 | tf_op jit(solution)/shard_map/ppermute | solution.py:20
  45.1 5.8 %collective-permute-start.9 = (f32[8,8,1,128]{3,0,2,1:T(8,128)S(1)}, f32[8,8,1,128]{3,0,2,1:T(8,128)S(1)}, u32[]{:S(2)}, u32[]{:S(2)}) collective-permute-start(f32[8,8,1,128]{3,0,2,1:T(8,128)S(1)} %get-tuple-element.15), channel_id=1, source_target_pairs={{2,0},{4,2},{6,4},{3,1},{5,3},{7,5},{10,8},{12,10},{14,12},{11,9},... | collective-permute-start | bytes 98312 | tf_op jit(solution)/shard_map/ppermute | solution.py:22
  51.6 1.6 collective-permute-start.11
  52.2 3.5 %collective-permute-start.10 = (f32[8,8,18,1]{2,1,3,0:T(8,128)S(1)}, f32[8,8,18,1]{2,1,3,0:T(8,128)S(1)}, u32[]{:S(2)}, u32[]{:S(2)}) collective-permute-start(f32[8,8,18,1]{2,1,3,0:T(8,128)S(1)} %copy.50), channel_id=1, source_target_pairs={{0,8},{8,16},{16,24},{24,0},{1,9},{9,17},{17,25},{25,1},{2,10},{10... | collective-permute-start | bytes 13832 | tf_op jit(solution)/shard_map/ppermute | solution.py:20
  78.0 41.8 %copy-start.1 = (f32[16,8,16,128]{3,0,2,1:T(8,128)S(1)}, f32[16,8,16,128]{3,0,2,1:T(8,128)}, u32[]{:S(2)}) copy-start(f32[16,8,16,128]{3,0,2,1:T(8,128)} %all-gather.2.cloned.1.call-done) | copy-start | bytes 3145732
  128.8 2.0 copy-start
Sparse Core Ops, SparseCore 0:
  58.4 19.4 all-gather.1
where the time goes:
time: 226 us; the launch traced here: 225 us
  blocking collectives  92.4 us (41%)
  waiting for transfers between devices  39.9 us (18%)
  matrix products  25.5 us (11%)
  local copies, waits for them, and re-layouts  18.7 us (8%)
  starting transfers between devices  17.6 us (8%)
  other arithmetic  16.8 us (7%)
  between operations  14.3 us (6%)
    psum x1, blocking collectives, shards(): lax.psum(product(grown, grown.T), ('lon', 'lat')) / total_cells  58.2 us
    psum x1, blocking collectives, shards(): lax.psum(product(columns, all_flat.T), ('lon', 'lat')) * inv_root  34.2 us
    all_gather x1, waiting for transfers between devices, shards(): gathered = lax.all_gather(smoothed, 'tm', axis=0, tiled=True)  19.6 us
    dot_general x3, matrix products, product(): jnp.dot(left, right, precision=lax.Precision.HIGHEST, preferred_element_t...  19.6 us
    ppermute x6, waiting for transfers between devices, with_halo(): lax.ppermute(head, axis, [((i + 1) % count, i) for i in range(ends)])  13.9 us
    ppermute x6, starting transfers between devices, with_halo(): lax.ppermute(tail, axis, [(i, (i + 1) % count) for i in range(ends)])  13.6 us
    unnamed x11, local copies, waits for them, and re-layouts  11.1 us
    another operation x3, other arithmetic, finish(): factor = jnp.linalg.cholesky(gram_matrix)  6.52 us
  transfers between devices with their start and end apart: 13, of which 13 were waited for; matrix products, arithmetic and copies ran while one was open for 1% of the time, Pallas kernels for 0%

commit v1 on v0

v1 whole, which is shorter than its diff:
```python
import functools
import math

import jax
import jax.numpy as jnp
from jax import lax
from jax.experimental import pallas as pl
from jax.experimental.pallas import tpu as pltpu
from jax.sharding import PartitionSpec as P

SMOOTH_RATE = 0.1
STEP_SIZE = 0.25
MESH = pl.DeviceIdType.MESH
W = 3
CONTRACT_LAST = (((1,), (1,)), ((), ()))


def split(values):
    high = values.astype(jnp.bfloat16)
    return high, (values - high.astype(jnp.float32)).astype(jnp.bfloat16)


def exact(left, right, dims=(((1,), (0,)), ((), ()))):
    return lax.dot_general(
        left, right, dims, precision=lax.Precision.HIGHEST, preferred_element_type=jnp.float32
    )


def smooth_rows(main, halo):
    lane = lax.broadcasted_iota(jnp.int32, (1,) + main.shape[1:], 2)
    level = lax.broadcasted_iota(jnp.int32, (1,) + main.shape[1:], 1)
    lanes, levels = main.shape[2], main.shape[1]
    mid_main, mid_halo = main[1:-1], halo[1:-1]
    main_lo, halo_lo = pltpu.roll(mid_main, 1, 2), pltpu.roll(mid_halo, 1, 2)
    main_hi, halo_hi = pltpu.roll(mid_main, lanes - 1, 2), pltpu.roll(mid_halo, lanes - 1, 2)
    first, last = lane == 0, lane == lanes - 1
    beside_main = jnp.where(first, halo_lo, main_lo) + jnp.where(last, halo_hi, main_hi)
    beside_halo = jnp.where(first, main_lo, halo_lo) + jnp.where(last, main_hi, halo_hi)

    def finish(whole, mid, beside):
        above = jnp.where(level == 0, 0.0, pltpu.roll(mid, 1, 1))
        below = jnp.where(level == levels - 1, 0.0, pltpu.roll(mid, levels - 1, 1))
        around = whole[2:] + whole[:-2] + beside + (above + below)
        return (1.0 - 6.0 * SMOOTH_RATE) * mid + SMOOTH_RATE * around

    return finish(main, mid_main, beside_main), finish(halo, mid_halo, beside_halo)


def edge_masked(rows, count, up_flag, down_flag):
    if count == 0:
        return rows
    return jnp.concatenate(
        [rows[:count] * up_flag, rows[count:-count], rows[-count:] * down_flag], axis=0
    )


def gather_kernel(
    sizes, snap_ref, q_hbm, red_ref, x_hbm,
    q_v, xm, xh, xs, pack, pack_in, corner, corner_in, z, sa, ra, rb, rc,
    q_sem, x_sem, halo_send, halo_recv, tm_send, tm_recv, a_send, a_recv, b_send, b_recv, c_send, c_recv,
):
    snaps, levels, rows, lanes, eofs, n_lon, n_lat, n_tm = sizes
    lon, lat, tm = lax.axis_index("lon"), lax.axis_index("lat"), lax.axis_index("tm")
    left, right = lax.rem(lon + n_lon - 1, n_lon), lax.rem(lon + 1, n_lon)
    group = n_lon * n_tm
    me = tm * n_lon + lon
    other = 1 - tm
    has_up, has_down = lat > 0, lat < n_lat - 1
    cells = rows * levels
    half = rows // n_tm

    q_copy = pltpu.make_async_copy(q_hbm, q_v, q_sem)
    q_copy.start()

    barrier = pltpu.get_barrier_semaphore()

    def greet(to_lon, to_lat, to_tm):
        pl.semaphore_signal(barrier, inc=1, device_id=(to_lon, to_lat, to_tm), device_id_type=MESH)

    def peer_of(distance):
        index = lax.rem(me + distance, group)
        return index, lax.rem(index, n_lon), index // n_lon

    for distance in range(1, group):
        _, to_lon, to_tm = peer_of(distance)
        greet(to_lon, lat, to_tm)
    for distance in range(1, n_lat):
        greet(lon, lax.rem(lat + distance, n_lat), tm)

    @pl.when(has_up)
    def _():
        greet(left, lat - 1, tm)
        greet(right, lat - 1, tm)

    @pl.when(has_down)
    def _():
        greet(left, lat + 1, tm)
        greet(right, lat + 1, tm)

    lane = lax.broadcasted_iota(jnp.int32, (levels, lanes), 1)

    def relayout(s, carry):
        to_left = jnp.zeros((levels, lanes), jnp.float32)
        to_right = jnp.zeros((levels, lanes), jnp.float32)
        for r in range(rows):
            field = snap_ref[pl.ds(s * cells + r, levels, stride=rows), :]
            xm[s, W + r] = field
            mine = (lane >= W * r) & (lane < W * (r + 1))
            low = field if r == 0 else pltpu.roll(field, W * r, 1)
            to_left = jnp.where(mine, low, to_left)
            to_right = jnp.where(mine, pltpu.roll(field, W * r + W, 1), to_right)
        pack[0, s] = to_left
        pack[1, s] = to_right
        return carry

    lax.fori_loop(0, snaps, relayout, 0)
    span = W * W
    for side in range(2):
        for end in range(2):
            start = 0 if end == 0 else W * (rows - W)
            packed = jnp.zeros((levels, lanes), jnp.float32)
            for s in range(snaps):
                shift = (span * s - start) % lanes
                moved = pack[side, s]
                moved = moved if shift == 0 else pltpu.roll(moved, shift, 1)
                packed = jnp.where((lane >= span * s) & (lane < span * (s + 1)), moved, packed)
            corner[2 * end + side] = packed

    pl.semaphore_wait(
        barrier,
        group - 1 + n_lat - 1 + 2 * has_up.astype(jnp.int32) + 2 * has_down.astype(jnp.int32),
    )

    def remote(src, dst, sends, recvs, slot, device):
        return pltpu.make_async_remote_copy(
            src_ref=src, dst_ref=dst, send_sem=sends.at[slot], recv_sem=recvs.at[slot],
            device_id=device, device_id_type=MESH,
        )

    to_left = remote(pack.at[0], pack_in.at[0], halo_send, halo_recv, 0, (left, lat, tm))
    to_right = remote(pack.at[1], pack_in.at[1], halo_send, halo_recv, 1, (right, lat, tm))
    up = [
        remote(xm.at[:, pl.ds(W, W)], xm.at[:, pl.ds(W + rows, W)], halo_send, halo_recv, 2, (lon, lat - 1, tm)),
        remote(corner.at[0], corner_in.at[0], halo_send, halo_recv, 3, (left, lat - 1, tm)),
        remote(corner.at[1], corner_in.at[1], halo_send, halo_recv, 4, (right, lat - 1, tm)),
    ]
    down = [
        remote(xm.at[:, pl.ds(rows, W)], xm.at[:, pl.ds(0, W)], halo_send, halo_recv, 5, (lon, lat + 1, tm)),
        remote(corner.at[2], corner_in.at[2], halo_send, halo_recv, 6, (left, lat + 1, tm)),
        remote(corner.at[3], corner_in.at[3], halo_send, halo_recv, 7, (right, lat + 1, tm)),
    ]

    @pl.when(has_up)
    def _():
        for copy in up:
            copy.start()

    @pl.when(has_down)
    def _():
        for copy in down:
            copy.start()

    to_left.start()
    to_right.start()

    @pl.when(jnp.logical_not(has_up))
    def _():
        xm[:, 0:W] = jnp.zeros((snaps, W, levels, lanes), jnp.float32)
        corner_in[2] = jnp.zeros((levels, lanes), jnp.float32)
        corner_in[3] = jnp.zeros((levels, lanes), jnp.float32)

    @pl.when(jnp.logical_not(has_down))
    def _():
        xm[:, W + rows :] = jnp.zeros((snaps, W, levels, lanes), jnp.float32)
        corner_in[0] = jnp.zeros((levels, lanes), jnp.float32)
        corner_in[1] = jnp.zeros((levels, lanes), jnp.float32)

    q_copy.wait()

    def basis_products(level, total):
        highs, lows = [], []
        for r in range(half):
            start = level * rows + tm * half + r
            high, low = split(q_v[pl.ds(start, eofs, stride=cells), :])
            highs.append(high)
            lows.append(low)
        part = jnp.concatenate(
            [jnp.concatenate(highs, axis=1), jnp.concatenate(lows, axis=1)], axis=0
        )
        z[0 : 2 * eofs, pl.ds(pl.multiple_of(level * (half * lanes), lanes), half * lanes)] = part
        return total + lax.dot_general(part, part, CONTRACT_LAST, preferred_element_type=jnp.float32)

    qq = lax.fori_loop(0, levels, basis_products, jnp.zeros((2 * eofs, 2 * eofs), jnp.float32))

    to_left.wait()
    to_right.wait()

    @pl.when(has_down)
    def _():
        up_in = [
            remote(xm.at[:, pl.ds(W, W)], xm.at[:, pl.ds(W + rows, W)], halo_send, halo_recv, 2, (lon, lat, tm)),
            remote(corner.at[0], corner_in.at[0], halo_send, halo_recv, 3, (lon, lat, tm)),
            remote(corner.at[1], corner_in.at[1], halo_send, halo_recv, 4, (lon, lat, tm)),
        ]
        for copy in up_in:
            copy.wait_recv()

    @pl.when(has_up)
    def _():
        down_in = [
            remote(xm.at[:, pl.ds(rows, W)], xm.at[:, pl.ds(0, W)], halo_send, halo_recv, 5, (lon, lat, tm)),
            remote(corner.at[2], corner_in.at[2], halo_send, halo_recv, 6, (lon, lat, tm)),
            remote(corner.at[3], corner_in.at[3], halo_send, halo_recv, 7, (lon, lat, tm)),
        ]
        for copy in down_in:
            copy.wait_recv()

    def beside(from_right, from_left, offset):
        low = from_right if offset == 0 else pltpu.roll(from_right, (lanes - offset) % lanes, 1)
        high = pltpu.roll(from_left, (lanes - W - offset) % lanes, 1)
        return jnp.where(lane < W, low, jnp.where(lane >= lanes - W, high, 0.0))

    for s in range(snaps):
        for j in range(W):
            offset = span * s + W * j
            xh[s, j] = beside(corner_in[2], corner_in[3], offset)
            xh[s, W + rows + j] = beside(corner_in[0], corner_in[1], offset)

    up_flag = has_up.astype(jnp.float32)
    down_flag = has_down.astype(jnp.float32)

    def tm_copy(s, part):
        where = pl.ds(tm * (snaps * cells) + s * cells + part * (half * levels), half * levels)
        first = part == other
        return where, first

    def share(s, part, slot):
        begin = pl.multiple_of(tm * (snaps * cells) + s * cells + part * (half * levels), levels)
        where = pl.ds(begin, half * levels)
        return remote(xs.at[where], xs.at[where], tm_send, tm_recv, slot, (lon, lat, other))

    def arrival(s, part, slot):
        begin = pl.multiple_of(other * (snaps * cells) + s * cells + part * (half * levels), levels)
        where = pl.ds(begin, half * levels)
        return remote(xs.at[where], xs.at[where], tm_send, tm_recv, slot, (lon, lat, other))

    def smooth(s, carry):
        for r in range(rows):
            xh[s, W + r] = beside(pack_in[0, s], pack_in[1, s], W * r)
        main, halo = xm[s], xh[s]
        for sweep in range(W):
            main, halo = smooth_rows(main, halo)
            main = edge_masked(main, W - 1 - sweep, up_flag, down_flag)
            halo = edge_masked(halo, W - 1 - sweep, up_flag, down_flag)
        begin = pl.multiple_of(tm * (snaps * cells) + s * cells, cells)
        xs[pl.ds(begin, cells), :] = main.reshape(cells, lanes)
        share(s, other, s).start()
        return carry

    lax.fori_loop(0, snaps, smooth, 0)
    for s in range(snaps):
        share(s, tm, snaps + s).start()
    own = pl.ds(pl.multiple_of(tm * (snaps * cells), cells), snaps * cells)
    others = pl.ds(pl.multiple_of(other * (snaps * cells), cells), snaps * cells)
    own_out = pltpu.make_async_copy(xs.at[own], x_hbm.at[own], x_sem.at[0])
    own_out.start()

    for s in range(snaps):
        arrival(s, tm, s).wait_recv()

    all_snaps = n_tm * snaps
    total_x = jnp.zeros((2 * eofs + 2 * all_snaps, 2 * all_snaps), jnp.float32)

    def snap_products(level, total):
        highs, lows = [], []
        for r in range(half):
            start = (tm * half + r) * levels + level
            high, low = split(xs[pl.ds(start, all_snaps, stride=cells), :])
            highs.append(high)
            lows.append(low)
        part = jnp.concatenate(
            [jnp.concatenate(highs, axis=1), jnp.concatenate(lows, axis=1)], axis=0
        )
        basis_part = z[:, pl.ds(pl.multiple_of(level * (half * lanes), lanes), half * lanes)]
        both = jnp.concatenate([basis_part, part], axis=0)
        return total + lax.dot_general(both, part, CONTRACT_LAST, preferred_element_type=jnp.float32)

    qx = lax.fori_loop(0, levels, snap_products, total_x)

    def fold(rows_of, count, width):
        added = rows_of[:count] + rows_of[count:]
        return added[:, :width] + added[:, width:]

    basis_gram = fold(qq, eofs, eofs)
    project = fold(qx[: 2 * eofs], eofs, all_snaps)
    snap_gram = fold(qx[2 * eofs :], all_snaps, all_snaps)
    snap_gram = jnp.concatenate(
        [snap_gram, jnp.zeros((eofs - all_snaps, all_snaps), jnp.float32)], axis=0
    )
    fill = jnp.zeros((eofs, lanes - eofs - 2 * all_snaps), jnp.float32)
    payload = jnp.concatenate([basis_gram, project, snap_gram, fill], axis=1)

    share_rows = eofs // group
    tile = sa.shape[1]
    for g in range(group):
        piece = payload[g * share_rows : (g + 1) * share_rows]
        if share_rows < tile:
            piece = jnp.concatenate(
                [piece, jnp.zeros((tile - share_rows, lanes), jnp.float32)], axis=0
            )
        sa[g] = piece
    a_copies = []
    for distance in range(1, group):
        index, to_lon, to_tm = peer_of(distance)
        copy = remote(sa.at[index], ra.at[distance], a_send, a_recv, distance, (to_lon, lat, to_tm))
        copy.start()
        a_copies.append(copy)
    partial = sa[me]
    for distance in range(1, group):
        a_copies[distance - 1].wait_recv()
        partial = partial + ra[distance]
    rb[lat] = partial
    b_copies = []
    for distance in range(1, n_lat):
        to_lat = lax.rem(lat + distance, n_lat)
        copy = remote(rb.at[lat], rb.at[lat], b_send, b_recv, distance, (lon, to_lat, tm))
        copy.start()
        b_copies.append(copy)
    for distance in range(1, n_lat):
        from_lat = lax.rem(lat + n_lat - distance, n_lat)
        remote(rb.at[from_lat], rb.at[from_lat], b_send, b_recv, distance, (lon, from_lat, tm)).wait_recv()
    for copy in b_copies:
        copy.wait_send()
    summed = rb[0]
    for index in range(1, n_lat):
        summed = summed + rb[index]
    rc[me] = summed
    c_copies = []
    for distance in range(1, group):
        _, to_lon, to_tm = peer_of(distance)
        copy = remote(rc.at[me], rc.at[me], c_send, c_recv, distance, (to_lon, lat, to_tm))
        copy.start()
        c_copies.append(copy)
    for distance in range(1, group):
        source = lax.rem(me + group - distance, group)
        remote(rc.at[source], rc.at[source], c_send, c_recv, distance, (lon, lat, other)).wait_recv()
    for copy in c_copies:
        copy.wait_send()
    for copy in a_copies:
        copy.wait_send()
    for g in range(group):
        red_ref[g * share_rows : (g + 1) * share_rows, :] = rc[g, 0:share_rows]

    for s in range(snaps):
        arrival(s, other, snaps + s).wait_recv()
    others_out = pltpu.make_async_copy(xs.at[others], x_hbm.at[others], x_sem.at[1])
    others_out.start()

    @pl.when(has_up)
    def _():
        for copy in up:
            copy.wait_send()

    @pl.when(has_down)
    def _():
        for copy in down:
            copy.wait_send()

    for s in range(snaps):
        share(s, other, s).wait_send()
        share(s, tm, snaps + s).wait_send()
    own_out.wait()
    others_out.wait()


def basis_kernel(sizes, red_ref, x_ref, q_hbm, out_hbm, coeff_ref, q_v, o_v, q_sem, o_sem):
    snaps, levels, rows, lanes, eofs, n_lon, n_lat, n_tm = sizes
    all_snaps = n_tm * snaps
    cells = rows * levels
    total_cells = cells * lanes * n_lon * n_lat
    inv_root = 1.0 / math.sqrt(total_cells)
    q_copy = pltpu.make_async_copy(q_hbm, q_v, q_sem)
    q_copy.start()

    sums = red_ref[...]
    coeffs = sums[:, eofs : eofs + all_snaps] * inv_root
    snap_gram = sums[0:all_snaps, eofs + all_snaps : eofs + 2 * all_snaps]
    inner = (2.0 * STEP_SIZE * inv_root) * coeffs + exact(
        coeffs, snap_gram * (STEP_SIZE * STEP_SIZE / total_cells)
    )
    gram = sums[:, 0:eofs] * (1.0 / total_cells) + exact(inner, coeffs, CONTRACT_LAST)
    coeff_ref[...] = coeffs

    row = lax.broadcasted_iota(jnp.int32, (eofs, eofs), 0)
    column = lax.broadcasted_iota(jnp.int32, (eofs, eofs), 1)
    joined = jnp.concatenate([gram, jnp.where(row == column, 1.0, 0.0)], axis=1)
    tiles = [joined[8 * j : 8 * j + 8] for j in range(eofs // 8)]
    sub = lax.broadcasted_iota(jnp.int32, (8, 1), 0)
    for k in range(eofs):
        j, i = divmod(k, 8)
        pivot_row = tiles[j][i : i + 1, :]
        scaled = pivot_row * (1.0 / pivot_row[:, k : k + 1])
        for t in range(j, eofs // 8):
            factor = tiles[t][:, k : k + 1]
            if t == j:
                factor = jnp.where(sub > i, factor, 0.0)
            tiles[t] = tiles[t] - factor * scaled
    joined = jnp.concatenate(tiles, axis=0)
    pivots = jnp.sum(jnp.where(row == column, joined[:, 0:eofs], 0.0), axis=1, keepdims=True)
    inverse = joined[:, eofs : 2 * eofs] * (1.0 / jnp.sqrt(pivots))
    mix = jnp.concatenate([inverse, STEP_SIZE * exact(inverse, coeffs)], axis=1)
    high = mix.astype(jnp.bfloat16).astype(jnp.float32)
    weights = jnp.concatenate([high, high, mix - high], axis=1).astype(jnp.bfloat16)

    q_copy.wait()
    out_rows = o_v.reshape(eofs * cells, lanes)

    def block(level):
        where = pl.ds(pl.multiple_of(level * rows, rows), rows)
        return pltpu.make_async_copy(o_v.at[:, where, :], out_hbm.at[:, where, :], o_sem.at[level])

    def one_level(level, carry):
        for r in range(0, rows, 2):
            highs, lows = [], []
            for n in (r, r + 1):
                q_high, q_low = split(q_v[pl.ds(level * rows + n, eofs, stride=cells), :])
                x_high, x_low = split(x_ref[pl.ds(n * levels + level, all_snaps, stride=cells), :])
                highs.append(jnp.concatenate([q_high, x_high], axis=0))
                lows.append(jnp.concatenate([q_low, x_low], axis=0))
            high = jnp.concatenate(highs, axis=1)
            low = jnp.concatenate(lows, axis=1)
            stack = jnp.concatenate([high, low, high], axis=0)
            result = jnp.dot(weights, stack, preferred_element_type=jnp.float32)
            out_rows[pl.ds(level * rows + r, eofs, stride=cells), :] = result[:, :lanes]
            out_rows[pl.ds(level * rows + r + 1, eofs, stride=cells), :] = result[:, lanes:]
        block(level).start()
        return carry

    lax.fori_loop(0, levels, one_level, 0)
    for level in range(levels):
        block(level).wait()


def shards(snapshots, basis):
    snaps, levels, rows, lanes = snapshots.shape
    eofs = basis.shape[0]
    n_lon, n_lat, n_tm = lax.axis_size("lon"), lax.axis_size("lat"), lax.axis_size("tm")
    sizes = (snaps, levels, rows, lanes, eofs, n_lon, n_lat, n_tm)
    cells = levels * rows
    group = n_lon * n_tm
    all_snaps = n_tm * snaps
    half = rows // n_tm
    tile = max(8, eofs // group)
    f32, bf16 = jnp.float32, jnp.bfloat16
    dma = pltpu.SemaphoreType.DMA
    vmem = pl.BlockSpec(memory_space=pltpu.VMEM)
    anywhere = pl.BlockSpec(memory_space=pl.ANY)
    flat = basis.reshape(eofs * cells, lanes)

    sums, smoothed = pl.pallas_call(
        functools.partial(gather_kernel, sizes),
        out_shape=(
            jax.ShapeDtypeStruct((eofs, lanes), f32),
            jax.ShapeDtypeStruct((all_snaps * cells, lanes), f32),
        ),
        in_specs=[vmem, anywhere],
        out_specs=(vmem, anywhere),
        scratch_shapes=[
            pltpu.VMEM((eofs * cells, lanes), f32),
            pltpu.VMEM((snaps, rows + 2 * W, levels, lanes), f32),
            pltpu.VMEM((snaps, rows + 2 * W, levels, lanes), f32),
            pltpu.VMEM((all_snaps * cells, lanes), f32),
            pltpu.VMEM((2, snaps, levels, lanes), f32),
            pltpu.VMEM((2, snaps, levels, lanes), f32),
            pltpu.VMEM((4, levels, lanes), f32),
            pltpu.VMEM((4, levels, lanes), f32),
            pltpu.VMEM((2 * eofs, levels * half * lanes), bf16),
            pltpu.VMEM((group, tile, lanes), f32),
            pltpu.VMEM((group, tile, lanes), f32),
            pltpu.VMEM((n_lat, tile, lanes), f32),
            pltpu.VMEM((group, tile, lanes), f32),
            dma,
            dma((2,)),
            dma((8,)),
            dma((8,)),
            dma((2 * snaps,)),
            dma((2 * snaps,)),
            dma((group,)),
            dma((group,)),
            dma((n_lat,)),
            dma((n_lat,)),
            dma((group,)),
            dma((group,)),
        ],
        compiler_params=pltpu.CompilerParams(
            collective_id=0, has_side_effects=True, vmem_limit_bytes=40 * 2**20
        ),
        name="smooth_and_sum",
    )(snapshots.reshape(snaps * cells, lanes), flat)

    new_basis, coeffs = pl.pallas_call(
        functools.partial(basis_kernel, sizes),
        out_shape=(
            jax.ShapeDtypeStruct((eofs, cells, lanes), f32),
            jax.ShapeDtypeStruct((eofs, all_snaps), f32),
        ),
        in_specs=[vmem, vmem, anywhere],
        out_specs=(anywhere, vmem),
        scratch_shapes=[
            pltpu.VMEM((eofs * cells, lanes), f32),
            pltpu.VMEM((eofs, cells, lanes), f32),
            dma,
            dma((levels,)),
        ],
        compiler_params=pltpu.CompilerParams(vmem_limit_bytes=40 * 2**20),
        name="update_basis",
    )(sums, smoothed, flat)
    own = lax.dynamic_slice_in_dim(coeffs, lax.axis_index("tm") * snaps, snaps, 1)
    return new_basis.reshape(basis.shape), own


def solution(mesh):
    placed = (P("tm", None, "lat", "lon"), P(None, None, "lat", "lon"))
    return jax.shard_map(
        shards,
        mesh=mesh,
        in_specs=placed,
        out_specs=(P(None, None, "lat", "lon"), P(None, "tm")),
        check_vma=False,
    )
```

time: 226 us -> 50.2 us (0.22)
  blocking collectives: 92.4 us -> 0 us
  Pallas kernels: 0 us -> 45.4 us
  waiting for transfers between devices: 39.9 us -> 0 us
  matrix products: 25.5 us -> 0 us
  starting transfers between devices: 17.6 us -> 0 us
  other arithmetic: 16.8 us -> 0 us
  local copies, waits for them, and re-layouts: 18.7 us -> 3.97 us
  between operations: 14.3 us -> 0.67 us
    psum x2 -> x0, blocking collectives: 92.4 us -> none  [the longest x1 58.2 us: shards(): lax.psum(product(grown, grown.T), ('lon', 'lat')) / total_cells]
    pallas_call x0 -> x2, Pallas kernels: none -> 45.4 us  [the longest x1 32.1 us: shards(): pl.pallas_call(functools.partial(gather_kernel, sizes), out_shape=(jax.Sh...]
    ppermute x12 -> x0, waiting for transfers between devices: 20.2 us -> none  [the longest x6 13.9 us: with_halo(): lax.ppermute(head, axis, [((i + 1) % count, i) for i in range(ends)])]
    all_gather x1 -> x0, waiting for transfers between devices: 19.6 us -> none  [shards(): gathered = lax.all_gather(smoothed, 'tm', axis=0, tiled=True)]
    dot_general x3 -> x0, matrix products: 19.6 us -> none  [product(): jnp.dot(left, right, precision=lax.Precision.HIGHEST, preferred_element_t...]
    ppermute x12 -> x0, starting transfers between devices: 17.6 us -> none  [the longest x6 13.6 us: with_halo(): lax.ppermute(tail, axis, [(i, (i + 1) % count) for i in range(ends)])]
    another operation x5 -> x0, other arithmetic: 12.1 us -> none  [the longest x3 6.52 us: finish(): factor = jnp.linalg.cholesky(gram_matrix)]
    unnamed x11 -> x7, local copies, waits for them, and re-layouts: 11.1 us -> 3.89 us
  transfers between devices with their start and end apart: 13 -> 0, of which waited for: 13 -> 0; matrix products, arithmetic and copies ran while one was open for 1% -> 0% of each run, Pallas kernels for 0% -> 0%
where the time goes in v1:
time: 50.2 us; the launch traced here: 50 us
  Pallas kernels  45.4 us (90%)
  local copies, waits for them, and re-layouts  3.97 us (8%)
  between operations  0.67 us (1%)
    pallas_call x1, Pallas kernels, shards(): pl.pallas_call(functools.partial(gather_kernel, sizes), out_shape=(jax.Sh...  32.1 us
    pallas_call x1, Pallas kernels, shards(): pl.pallas_call(functools.partial(basis_kernel, sizes), out_shape=(jax.Sha...  13.3 us
    unnamed x7, local copies, waits for them, and re-layouts  3.89 us

profile of v1, /device:TPU:0, one launch (start us, length us, event | category | flops | bytes accessed | tf_op | source)
XLA Modules:
  0.0 50.0 jit_solution(15160777187705337870)
XLA Ops:
  0.6 0.0 copy-start
  0.6 2.2 %copy-done = f32[64,8,16,128]{3,2,1,0:T(8,128)S(1)} copy-done((f32[64,8,16,128]{3,2,1,0:T(8,128)S(1)}, f32[64,8,16,128]{3,2,1,0:T(8,128)}, u32[]{:S(2)}) %copy-start) | copy-done | bytes 4194328
  2.8 0.0 copy-start.2
  2.8 1.0 %copy-done.2 = f32[8,8,16,128]{3,2,1,0:T(8,128)S(1)} copy-done((f32[8,8,16,128]{3,2,1,0:T(8,128)S(1)}, f32[8,8,16,128]{3,2,1,0:T(8,128)}, u32[]{:S(2)}) %copy-start.2) | copy-done | bytes 524312
  3.9 0.0 copy-start.1
  3.9 32.1 %smooth_and_sum.1 = (f32[64,128]{1,0:T(8,128)S(1)}, f32[2048,128]{1,0:T(8,128)S(1)}) custom-call(f32[1024,128]{1,0:T(8,128)S(1)} %bitcast.5, f32[8192,128]{1,0:T(8,128)S(1)} %bitcast.3), custom_call_target="tpu_custom_call" | custom-call | tf_op jit(solution)/shard_map/smooth_and_sum/pallas_call | solution.py:460
  36.0 0.0 copy-done.1
  36.0 13.3 %update_basis.1 = (f32[64,128,128]{2,1,0:T(8,128)}, f32[64,16]{1,0:T(8,128)S(1)}) custom-call(f32[64,128]{1,0:T(8,128)S(1)} %get-tuple-element.6.red_ref, f32[2048,128]{1,0:T(8,128)S(1)} %get-tuple-element.7.x_ref, f32[8192,128]{1,0:T(8,128)S(1)} %bitcast.4), custom_call_target="tpu_custom_call" | custom-call | tf_op jit(solution)/shard_map/update_basis/pallas_call | solution.py:501
  49.3 0.1 constant_dynamic-slice_fusion
  49.3 0.7 %copy.4 = f32[64,8]{0,1:T(8,128)} copy(f32[64,8]{1,0:T(8,128)S(1)} %constant_dynamic-slice_fusion) | data formatting | bytes 4096
Async XLA Ops:
  0.6 2.2 %copy-start = (f32[64,8,16,128]{3,2,1,0:T(8,128)S(1)}, f32[64,8,16,128]{3,2,1,0:T(8,128)}, u32[]{:S(2)}) copy-start(f32[64,8,16,128]{3,2,1,0:T(8,128)} %param.3) | copy-start | bytes 12582916
  2.8 1.0 %copy-start.2 = (f32[8,8,16,128]{3,2,1,0:T(8,128)S(1)}, f32[8,8,16,128]{3,2,1,0:T(8,128)}, u32[]{:S(2)}) copy-start(f32[8,8,16,128]{3,2,1,0:T(8,128)} %param.2) | copy-start | bytes 1572868
  3.9 32.1 %copy-start.1 = (f32[64,8,16,128]{3,2,1,0:T(8,128)S(1)}, f32[64,8,16,128]{3,2,1,0:T(8,128)}, u32[]{:S(2)}) copy-start(f32[64,8,16,128]{3,2,1,0:T(8,128)} %param.3) | copy-start | bytes 12582916

commit v2 on v1

--- a/solution.py
+++ b/solution.py
@@ -54,9 +54,44 @@
     )
 
 
+def update_weights(sums, eofs, all_snaps, total_cells):
+    inv_root = 1.0 / math.sqrt(total_cells)
+    coeffs = sums[:, eofs : eofs + all_snaps] * inv_root
+    snap_gram = sums[0:all_snaps, eofs + all_snaps : eofs + 2 * all_snaps]
+    inner = (2.0 * STEP_SIZE * inv_root) * coeffs + exact(
+        coeffs, snap_gram * (STEP_SIZE * STEP_SIZE / total_cells)
+    )
+    gram = sums[:, 0:eofs] * (1.0 / total_cells) + exact(inner, coeffs, CONTRACT_LAST)
+
+    block = 8
+    row = lax.broadcasted_iota(jnp.int32, (eofs, eofs), 0)
+    column = lax.broadcasted_iota(jnp.int32, (eofs, eofs), 1)
+    rest = jnp.concatenate([gram, jnp.where(row == column, 1.0, 0.0)], axis=1)
+    done = []
+    for first in range(0, eofs, block):
+        place = lax.broadcasted_iota(jnp.int32, rest.shape, 0)
+        spread = [
+            jnp.broadcast_to(rest[:, first + i : first + i + 1], rest.shape) for i in range(block)
+        ]
+        pivots = jnp.ones((block, rest.shape[1]), jnp.float32)
+        for i in range(block):
+            pivot = spread[i][i : i + 1, :]
+            pivots = jnp.where(place[:block] == i, pivot, pivots)
+            factor = jnp.where(place > i, spread[i], 0.0) * (1.0 / pivot)
+            for n in range(i + 1, block):
+                spread[n] = spread[n] - factor * spread[i][n : n + 1, :]
+            rest = rest - factor * rest[i : i + 1, :]
+        done.append(rest[:block] * (1.0 / jnp.sqrt(pivots)))
+        rest = rest[block:]
+    inverse = jnp.concatenate(done, axis=0)[:, eofs : 2 * eofs]
+    mix = jnp.concatenate([inverse, STEP_SIZE * exact(inverse, coeffs)], axis=1)
+    high = mix.astype(jnp.bfloat16).astype(jnp.float32)
+    return coeffs, jnp.concatenate([high, high, mix - high], axis=1).astype(jnp.bfloat16)
+
+
 def gather_kernel(
-    sizes, snap_ref, q_hbm, red_ref, x_hbm,
-    q_v, xm, xh, xs, pack, pack_in, corner, corner_in, z, sa, ra, rb, rc,
+    sizes, snap_hbm, q_hbm, weight_ref, coeff_ref, z,
+    snap_ref, q_v, xm, xh, xs, pack, pack_in, corner, corner_in, sa, ra, rb, rc,
     q_sem, x_sem, halo_send, halo_recv, tm_send, tm_recv, a_send, a_recv, b_send, b_recv, c_send, c_recv,
 ):
     snaps, levels, rows, lanes, eofs, n_lon, n_lat, n_tm = sizes
@@ -69,6 +104,8 @@
     cells = rows * levels
     half = rows // n_tm
 
+    snap_copy = pltpu.make_async_copy(snap_hbm, snap_ref, x_sem)
+    snap_copy.start()
     q_copy = pltpu.make_async_copy(q_hbm, q_v, q_sem)
     q_copy.start()
 
@@ -113,6 +150,7 @@
         pack[1, s] = to_right
         return carry
 
+    snap_copy.wait()
     lax.fori_loop(0, snaps, relayout, 0)
     span = W * W
     for side in range(2):
@@ -176,18 +214,35 @@
         corner_in[1] = jnp.zeros((levels, lanes), jnp.float32)
 
     q_copy.wait()
-
-    def basis_products(level, total):
+    all_snaps = n_tm * snaps
+    joint = eofs + all_snaps
+    wide = half * lanes
+
+    def columns(part, level):
+        return pl.ds(pl.multiple_of((part * levels + level) * wide, lanes), wide)
+
+    def split_rows(ref, count, start, step):
         highs, lows = [], []
         for r in range(half):
-            start = level * rows + tm * half + r
-            high, low = split(q_v[pl.ds(start, eofs, stride=cells), :])
+            high, low = split(ref[pl.ds(start + r * step, count, stride=cells), :])
             highs.append(high)
             lows.append(low)
-        part = jnp.concatenate(
-            [jnp.concatenate(highs, axis=1), jnp.concatenate(lows, axis=1)], axis=0
-        )
-        z[0 : 2 * eofs, pl.ds(pl.multiple_of(level * (half * lanes), lanes), half * lanes)] = part
+        return jnp.concatenate(highs, axis=1), jnp.concatenate(lows, axis=1)
+
+    def place_basis(part, level):
+        high, low = split_rows(q_v, eofs, level * rows + part * half, 1)
+        z[0:eofs, columns(part, level)] = high
+        z[joint : joint + eofs, columns(part, level)] = low
+        return jnp.concatenate([high, low], axis=0)
+
+    def place_snaps(part, level):
+        high, low = split_rows(xs, all_snaps, part * half * levels + level, levels)
+        z[eofs:joint, columns(part, level)] = high
+        z[joint + eofs : 2 * joint, columns(part, level)] = low
+        return jnp.concatenate([high, low], axis=0)
+
+    def basis_products(level, total):
+        part = place_basis(tm, level)
         return total + lax.dot_general(part, part, CONTRACT_LAST, preferred_element_type=jnp.float32)
 
     qq = lax.fori_loop(0, levels, basis_products, jnp.zeros((2 * eofs, 2 * eofs), jnp.float32))
@@ -228,11 +283,6 @@
 
     up_flag = has_up.astype(jnp.float32)
     down_flag = has_down.astype(jnp.float32)
-
-    def tm_copy(s, part):
-        where = pl.ds(tm * (snaps * cells) + s * cells + part * (half * levels), half * levels)
-        first = part == other
-        return where, first
 
     def share(s, part, slot):
         begin = pl.multiple_of(tm * (snaps * cells) + s * cells + part * (half * levels), levels)
@@ -258,42 +308,39 @@
         return carry
 
     lax.fori_loop(0, snaps, smooth, 0)
-    for s in range(snaps):
-        share(s, tm, snaps + s).start()
-    own = pl.ds(pl.multiple_of(tm * (snaps * cells), cells), snaps * cells)
-    others = pl.ds(pl.multiple_of(other * (snaps * cells), cells), snaps * cells)
-    own_out = pltpu.make_async_copy(xs.at[own], x_hbm.at[own], x_sem.at[0])
-    own_out.start()
+    early, middle = snaps // 4, (5 * snaps) // 8
+
+    def share_rest(begin, end):
+        for s in range(begin, end):
+            share(s, tm, snaps + s).start()
+
+    share_rest(0, early)
+
+    def place_rest(level, carry):
+        place_basis(other, level)
+        return carry
+
+    lax.fori_loop(0, levels, place_rest, 0)
 
     for s in range(snaps):
         arrival(s, tm, s).wait_recv()
 
-    all_snaps = n_tm * snaps
-    total_x = jnp.zeros((2 * eofs + 2 * all_snaps, 2 * all_snaps), jnp.float32)
-
     def snap_products(level, total):
-        highs, lows = [], []
-        for r in range(half):
-            start = (tm * half + r) * levels + level
-            high, low = split(xs[pl.ds(start, all_snaps, stride=cells), :])
-            highs.append(high)
-            lows.append(low)
-        part = jnp.concatenate(
-            [jnp.concatenate(highs, axis=1), jnp.concatenate(lows, axis=1)], axis=0
-        )
-        basis_part = z[:, pl.ds(pl.multiple_of(level * (half * lanes), lanes), half * lanes)]
-        both = jnp.concatenate([basis_part, part], axis=0)
+        part = place_snaps(tm, level)
+        both = z[:, columns(tm, level)]
         return total + lax.dot_general(both, part, CONTRACT_LAST, preferred_element_type=jnp.float32)
 
-    qx = lax.fori_loop(0, levels, snap_products, total_x)
+    qx = lax.fori_loop(
+        0, levels, snap_products, jnp.zeros((2 * joint, 2 * all_snaps), jnp.float32)
+    )
 
     def fold(rows_of, count, width):
         added = rows_of[:count] + rows_of[count:]
         return added[:, :width] + added[:, width:]
 
     basis_gram = fold(qq, eofs, eofs)
-    project = fold(qx[: 2 * eofs], eofs, all_snaps)
-    snap_gram = fold(qx[2 * eofs :], all_snaps, all_snaps)
+    with_snaps = fold(qx, joint, all_snaps)
+    project, snap_gram = with_snaps[:eofs], with_snaps[eofs:]
     snap_gram = jnp.concatenate(
         [snap_gram, jnp.zeros((eofs - all_snaps, all_snaps), jnp.float32)], axis=0
     )
@@ -326,6 +373,7 @@
         copy = remote(rb.at[lat], rb.at[lat], b_send, b_recv, distance, (lon, to_lat, tm))
         copy.start()
         b_copies.append(copy)
+    share_rest(early, middle)
     for distance in range(1, n_lat):
         from_lat = lax.rem(lat + n_lat - distance, n_lat)
         remote(rb.at[from_lat], rb.at[from_lat], b_send, b_recv, distance, (lon, from_lat, tm)).wait_recv()
@@ -341,20 +389,26 @@
         copy = remote(rc.at[me], rc.at[me], c_send, c_recv, distance, (to_lon, lat, to_tm))
         copy.start()
         c_copies.append(copy)
+    share_rest(middle, snaps)
     for distance in range(1, group):
         source = lax.rem(me + group - distance, group)
         remote(rc.at[source], rc.at[source], c_send, c_recv, distance, (lon, lat, other)).wait_recv()
-    for copy in c_copies:
-        copy.wait_send()
-    for copy in a_copies:
-        copy.wait_send()
-    for g in range(group):
-        red_ref[g * share_rows : (g + 1) * share_rows, :] = rc[g, 0:share_rows]
+    sums = jnp.concatenate([rc[g, 0:share_rows] for g in range(group)], axis=0)
+    coeffs, weights = update_weights(sums, eofs, all_snaps, cells * lanes * n_lon * n_lat)
+    coeff_ref[...] = coeffs
+    weight_ref[...] = weights
 
     for s in range(snaps):
         arrival(s, other, snaps + s).wait_recv()
-    others_out = pltpu.make_async_copy(xs.at[others], x_hbm.at[others], x_sem.at[1])
-    others_out.start()
+
+    def place_last(level, carry):
+        place_snaps(other, level)
+        return carry
+
+    lax.fori_loop(0, levels, place_last, 0)
+
+    for copy in a_copies + c_copies:
+        copy.wait_send()
 
     @pl.when(has_up)
     def _():
@@ -369,76 +423,42 @@
     for s in range(snaps):
         share(s, other, s).wait_send()
         share(s, tm, snaps + s).wait_send()
-    own_out.wait()
-    others_out.wait()
-
-
-def basis_kernel(sizes, red_ref, x_ref, q_hbm, out_hbm, coeff_ref, q_v, o_v, q_sem, o_sem):
+
+
+def basis_kernel(sizes, weight_ref, coeff_ref, z, out_hbm, own_ref, o_v, o_sem):
     snaps, levels, rows, lanes, eofs, n_lon, n_lat, n_tm = sizes
     all_snaps = n_tm * snaps
+    joint = eofs + all_snaps
     cells = rows * levels
-    total_cells = cells * lanes * n_lon * n_lat
-    inv_root = 1.0 / math.sqrt(total_cells)
-    q_copy = pltpu.make_async_copy(q_hbm, q_v, q_sem)
-    q_copy.start()
-
-    sums = red_ref[...]
-    coeffs = sums[:, eofs : eofs + all_snaps] * inv_root
-    snap_gram = sums[0:all_snaps, eofs + all_snaps : eofs + 2 * all_snaps]
-    inner = (2.0 * STEP_SIZE * inv_root) * coeffs + exact(
-        coeffs, snap_gram * (STEP_SIZE * STEP_SIZE / total_cells)
-    )
-    gram = sums[:, 0:eofs] * (1.0 / total_cells) + exact(inner, coeffs, CONTRACT_LAST)
-    coeff_ref[...] = coeffs
-
-    row = lax.broadcasted_iota(jnp.int32, (eofs, eofs), 0)
-    column = lax.broadcasted_iota(jnp.int32, (eofs, eofs), 1)
-    joined = jnp.concatenate([gram, jnp.where(row == column, 1.0, 0.0)], axis=1)
-    tiles = [joined[8 * j : 8 * j + 8] for j in range(eofs // 8)]
-    sub = lax.broadcasted_iota(jnp.int32, (8, 1), 0)
-    for k in range(eofs):
-        j, i = divmod(k, 8)
-        pivot_row = tiles[j][i : i + 1, :]
-        scaled = pivot_row * (1.0 / pivot_row[:, k : k + 1])
-        for t in range(j, eofs // 8):
-            factor = tiles[t][:, k : k + 1]
-            if t == j:
-                factor = jnp.where(sub > i, factor, 0.0)
-            tiles[t] = tiles[t] - factor * scaled
-    joined = jnp.concatenate(tiles, axis=0)
-    pivots = jnp.sum(jnp.where(row == column, joined[:, 0:eofs], 0.0), axis=1, keepdims=True)
-    inverse = joined[:, eofs : 2 * eofs] * (1.0 / jnp.sqrt(pivots))
-    mix = jnp.concatenate([inverse, STEP_SIZE * exact(inverse, coeffs)], axis=1)
-    high = mix.astype(jnp.bfloat16).astype(jnp.float32)
-    weights = jnp.concatenate([high, high, mix - high], axis=1).astype(jnp.bfloat16)
-
-    q_copy.wait()
+    half = rows // n_tm
+    wide = half * lanes
     out_rows = o_v.reshape(eofs * cells, lanes)
-
-    def block(level):
-        where = pl.ds(pl.multiple_of(level * rows, rows), rows)
-        return pltpu.make_async_copy(o_v.at[:, where, :], out_hbm.at[:, where, :], o_sem.at[level])
-
-    def one_level(level, carry):
-        for r in range(0, rows, 2):
-            highs, lows = [], []
-            for n in (r, r + 1):
-                q_high, q_low = split(q_v[pl.ds(level * rows + n, eofs, stride=cells), :])
-                x_high, x_low = split(x_ref[pl.ds(n * levels + level, all_snaps, stride=cells), :])
-                highs.append(jnp.concatenate([q_high, x_high], axis=0))
-                lows.append(jnp.concatenate([q_low, x_low], axis=0))
-            high = jnp.concatenate(highs, axis=1)
-            low = jnp.concatenate(lows, axis=1)
-            stack = jnp.concatenate([high, low, high], axis=0)
+    weights = weight_ref[...]
+
+    def block(step):
+        part, level = step // levels, lax.rem(step, levels)
+        where = pl.ds(pl.multiple_of(level * rows + part * half, half), half)
+        return pltpu.make_async_copy(o_v.at[:, where, :], out_hbm.at[:, where, :], o_sem.at[step])
+
+    def one_block(step, carry):
+        part, level = step // levels, lax.rem(step, levels)
+        for r in range(0, half, 2):
+            begin = pl.multiple_of(step * wide + r * lanes, lanes)
+            where = pl.ds(begin, 2 * lanes)
+            stack = jnp.concatenate([z[:, where], z[0:joint, where]], axis=0)
             result = jnp.dot(weights, stack, preferred_element_type=jnp.float32)
-            out_rows[pl.ds(level * rows + r, eofs, stride=cells), :] = result[:, :lanes]
-            out_rows[pl.ds(level * rows + r + 1, eofs, stride=cells), :] = result[:, lanes:]
-        block(level).start()
+            start = level * rows + part * half + r
+            out_rows[pl.ds(start, eofs, stride=cells), :] = result[:, :lanes]
+            out_rows[pl.ds(start + 1, eofs, stride=cells), :] = result[:, lanes:]
+        block(step).start()
         return carry
 
-    lax.fori_loop(0, levels, one_level, 0)
-    for level in range(levels):
-        block(level).wait()
+    lax.fori_loop(0, n_tm * levels, one_block, 0)
+    chosen = lax.broadcasted_iota(jnp.int32, (snaps, all_snaps), 0) + lax.axis_index("tm") * snaps
+    column = lax.broadcasted_iota(jnp.int32, (snaps, all_snaps), 1)
+    own_ref[...] = exact(jnp.where(chosen == column, 1.0, 0.0), coeff_ref[...], CONTRACT_LAST)
+    for step in range(n_tm * levels):
+        block(step).wait()
 
 
 def shards(snapshots, basis):
@@ -449,23 +469,25 @@
     cells = levels * rows
     group = n_lon * n_tm
     all_snaps = n_tm * snaps
-    half = rows // n_tm
+    joint = eofs + all_snaps
     tile = max(8, eofs // group)
     f32, bf16 = jnp.float32, jnp.bfloat16
     dma = pltpu.SemaphoreType.DMA
     vmem = pl.BlockSpec(memory_space=pltpu.VMEM)
-    anywhere = pl.BlockSpec(memory_space=pl.ANY)
+    in_hbm = pl.BlockSpec(memory_space=pltpu.HBM)
     flat = basis.reshape(eofs * cells, lanes)
 
-    sums, smoothed = pl.pallas_call(
+    weights, coeffs, parts = pl.pallas_call(
         functools.partial(gather_kernel, sizes),
         out_shape=(
-            jax.ShapeDtypeStruct((eofs, lanes), f32),
-            jax.ShapeDtypeStruct((all_snaps * cells, lanes), f32),
+            jax.ShapeDtypeStruct((eofs, 3 * joint), bf16),
+            jax.ShapeDtypeStruct((eofs, all_snaps), f32),
+            jax.ShapeDtypeStruct((2 * joint, cells * lanes), bf16),
         ),
-        in_specs=[vmem, anywhere],
-        out_specs=(vmem, anywhere),
+        in_specs=[in_hbm, in_hbm],
+        out_specs=(vmem, vmem, vmem),
         scratch_shapes=[
+            pltpu.VMEM((snaps * cells, lanes), f32),
             pltpu.VMEM((eofs * cells, lanes), f32),
             pltpu.VMEM((snaps, rows + 2 * W, levels, lanes), f32),
             pltpu.VMEM((snaps, rows + 2 * W, levels, lanes), f32),
@@ -474,13 +496,12 @@
             pltpu.VMEM((2, snaps, levels, lanes), f32),
             pltpu.VMEM((4, levels, lanes), f32),
             pltpu.VMEM((4, levels, lanes), f32),
-            pltpu.VMEM((2 * eofs, levels * half * lanes), bf16),
             pltpu.VMEM((group, tile, lanes), f32),
             pltpu.VMEM((group, tile, lanes), f32),
             pltpu.VMEM((n_lat, tile, lanes), f32),
             pltpu.VMEM((group, tile, lanes), f32),
             dma,
-            dma((2,)),
+            dma,
             dma((8,)),
             dma((8,)),
             dma((2 * snaps,)),
@@ -496,27 +517,27 @@
             collective_id=0, has_side_effects=True, vmem_limit_bytes=40 * 2**20
         ),
         name="smooth_and_sum",
-    )(snapshots.reshape(snaps * cells, lanes), flat)
-
-    new_basis, coeffs = pl.pallas_call(
+    )(
+        pltpu.with_memory_space_constraint(snapshots.reshape(snaps * cells, lanes), pltpu.HBM),
+        pltpu.with_memory_space_constraint(flat, pltpu.HBM),
+    )
+
+    new_basis, own = pl.pallas_call(
         functools.partial(basis_kernel, sizes),
         out_shape=(
             jax.ShapeDtypeStruct((eofs, cells, lanes), f32),
-            jax.ShapeDtypeStruct((eofs, all_snaps), f32),
+            jax.ShapeDtypeStruct((snaps, eofs), f32),
         ),
-        in_specs=[vmem, vmem, anywhere],
-        out_specs=(anywhere, vmem),
+        in_specs=[vmem, vmem, vmem],
+        out_specs=(in_hbm, vmem),
         scratch_shapes=[
-            pltpu.VMEM((eofs * cells, lanes), f32),
             pltpu.VMEM((eofs, cells, lanes), f32),
-            dma,
-            dma((levels,)),
+            dma((n_tm * levels,)),
         ],
-        compiler_params=pltpu.CompilerParams(vmem_limit_bytes=40 * 2**20),
+        compiler_params=pltpu.CompilerParams(vmem_limit_bytes=32 * 2**20),
         name="update_basis",
-    )(sums, smoothed, flat)
-    own = lax.dynamic_slice_in_dim(coeffs, lax.axis_index("tm") * snaps, snaps, 1)
-    return new_basis.reshape(basis.shape), own
+    )(weights, coeffs, parts)
+    return new_basis.reshape(basis.shape), own.T
 
 
 def solution(mesh):

time: 50.2 us -> 42 us (0.84)
  Pallas kernels: 45.4 us -> 41.2 us
  local copies, waits for them, and re-layouts: 3.97 us -> 0 us
    pallas_call x1, Pallas kernels: 13.3 us -> 6.53 us  [shards(): pl.pallas_call(functools.partial(basis_kernel, sizes), out_shape=(jax.Sha...]
    unnamed x7 -> x0, local copies, waits for them, and re-layouts: 3.89 us -> none
    pallas_call x1, Pallas kernels: 32.1 us -> 34.6 us  [shards(): pl.pallas_call(functools.partial(gather_kernel, sizes), out_shape=(jax.Sh...]
where the time goes in v2:
time: 42 us; the launch traced here: 41.8 us
  Pallas kernels  41.2 us (98%)
  between operations  0.64 us (2%)
    pallas_call x1, Pallas kernels, shards(): pl.pallas_call(functools.partial(gather_kernel, sizes), out_shape=(jax.Sh...  34.6 us
    pallas_call x1, Pallas kernels, shards(): pl.pallas_call(functools.partial(basis_kernel, sizes), out_shape=(jax.Sha...  6.53 us

profile of v2, /device:TPU:0, one launch (start us, length us, event | category | flops | bytes accessed | tf_op | source)
XLA Modules:
  0.0 41.8 jit_solution(4169253154493294672)
XLA Ops:
  0.6 34.6 %smooth_and_sum.1 = (bf16[64,240]{1,0:T(8,128)(2,1)S(1)}, f32[64,16]{1,0:T(8,128)S(1)}, bf16[160,16384]{1,0:T(8,128)(2,1)S(1)}) custom-call(f32[1024,128]{1,0:T(8,128)} %bitcast.5, f32[8192,128]{1,0:T(8,128)} %bitcast.4), custom_call_target="tpu_custom_call" | custom-call | tf_op jit(solution)/shard_map/smooth_and_sum/pallas_call | solution.py:480
  35.3 6.5 %update_basis.1 = (f32[64,128,128]{2,1,0:T(8,128)}, f32[8,64]{1,0:T(8,128)}) custom-call(bf16[64,240]{1,0:T(8,128)(2,1)S(1)} %get-tuple-element.7.weight_ref, f32[64,16]{1,0:T(8,128)S(1)} %get-tuple-element.8.coeff_ref, bf16[160,16384]{1,0:T(8,128)(2,1)S(1)} %get-tuple-element.9.z), custom_call_target="tpu_custom_call" | custom-call | tf_op jit(solution)/shard_map/update_basis/pallas_call | solution.py:525

commit v3 on v2

--- a/solution.py
+++ b/solution.py
@@ -241,11 +241,19 @@
         z[joint + eofs : 2 * joint, columns(part, level)] = low
         return jnp.concatenate([high, low], axis=0)
 
-    def basis_products(level, total):
-        part = place_basis(tm, level)
-        return total + lax.dot_general(part, part, CONTRACT_LAST, preferred_element_type=jnp.float32)
-
-    qq = lax.fori_loop(0, levels, basis_products, jnp.zeros((2 * eofs, 2 * eofs), jnp.float32))
+    run = 4 if levels % 4 == 0 else 1
+
+    def basis_products(step, total):
+        for level in range(run):
+            part = place_basis(tm, step * run + level)
+            total = total + lax.dot_general(
+                part, part, CONTRACT_LAST, preferred_element_type=jnp.float32
+            )
+        return total
+
+    qq = lax.fori_loop(
+        0, levels // run, basis_products, jnp.zeros((2 * eofs, 2 * eofs), jnp.float32)
+    )
 
     to_left.wait()
     to_right.wait()
@@ -316,23 +324,21 @@
 
     share_rest(0, early)
 
-    def place_rest(level, carry):
-        place_basis(other, level)
+    def place_rest(step, carry):
+        for level in range(run):
+            place_basis(other, step * run + level)
         return carry
 
-    lax.fori_loop(0, levels, place_rest, 0)
+    lax.fori_loop(0, levels // run, place_rest, 0)
 
     for s in range(snaps):
         arrival(s, tm, s).wait_recv()
 
-    def snap_products(level, total):
+    qx = jnp.zeros((2 * joint, 2 * all_snaps), jnp.float32)
+    for level in range(levels):
         part = place_snaps(tm, level)
         both = z[:, columns(tm, level)]
-        return total + lax.dot_general(both, part, CONTRACT_LAST, preferred_element_type=jnp.float32)
-
-    qx = lax.fori_loop(
-        0, levels, snap_products, jnp.zeros((2 * joint, 2 * all_snaps), jnp.float32)
-    )
+        qx = qx + lax.dot_general(both, part, CONTRACT_LAST, preferred_element_type=jnp.float32)
 
     def fold(rows_of, count, width):
         added = rows_of[:count] + rows_of[count:]
@@ -401,11 +407,8 @@
     for s in range(snaps):
         arrival(s, other, snaps + s).wait_recv()
 
-    def place_last(level, carry):
+    for level in range(levels):
         place_snaps(other, level)
-        return carry
-
-    lax.fori_loop(0, levels, place_last, 0)
 
     for copy in a_copies + c_copies:
         copy.wait_send()
@@ -440,20 +443,24 @@
         where = pl.ds(pl.multiple_of(level * rows + part * half, half), half)
         return pltpu.make_async_copy(o_v.at[:, where, :], out_hbm.at[:, where, :], o_sem.at[step])
 
-    def one_block(step, carry):
-        part, level = step // levels, lax.rem(step, levels)
-        for r in range(0, half, 2):
-            begin = pl.multiple_of(step * wide + r * lanes, lanes)
-            where = pl.ds(begin, 2 * lanes)
-            stack = jnp.concatenate([z[:, where], z[0:joint, where]], axis=0)
-            result = jnp.dot(weights, stack, preferred_element_type=jnp.float32)
-            start = level * rows + part * half + r
-            out_rows[pl.ds(start, eofs, stride=cells), :] = result[:, :lanes]
-            out_rows[pl.ds(start + 1, eofs, stride=cells), :] = result[:, lanes:]
-        block(step).start()
+    run = 4 if levels % 4 == 0 else 1
+
+    def one_run(index, carry):
+        for inner in range(run):
+            step = index * run + inner
+            part, level = step // levels, lax.rem(step, levels)
+            for r in range(0, half, 2):
+                begin = pl.multiple_of(step * wide + r * lanes, lanes)
+                where = pl.ds(begin, 2 * lanes)
+                stack = jnp.concatenate([z[:, where], z[0:joint, where]], axis=0)
+                result = jnp.dot(weights, stack, preferred_element_type=jnp.float32)
+                start = level * rows + part * half + r
+                out_rows[pl.ds(start, eofs, stride=cells), :] = result[:, :lanes]
+                out_rows[pl.ds(start + 1, eofs, stride=cells), :] = result[:, lanes:]
+            block(step).start()
         return carry
 
-    lax.fori_loop(0, n_tm * levels, one_block, 0)
+    lax.fori_loop(0, n_tm * levels // run, one_run, 0)
     chosen = lax.broadcasted_iota(jnp.int32, (snaps, all_snaps), 0) + lax.axis_index("tm") * snaps
     column = lax.broadcasted_iota(jnp.int32, (snaps, all_snaps), 1)
     own_ref[...] = exact(jnp.where(chosen == column, 1.0, 0.0), coeff_ref[...], CONTRACT_LAST)

time: 42 us -> 39.3 us (0.936)
  Pallas kernels: 41.2 us -> 38.5 us
    pallas_call x1, Pallas kernels: 6.53 us -> 4.98 us  [shards(): pl.pallas_call(functools.partial(basis_kernel, sizes), out_shape=(jax.Sha...]
    pallas_call x1, Pallas kernels: 34.6 us -> 33.5 us  [shards(): pl.pallas_call(functools.partial(gather_kernel, sizes), out_shape=(jax.Sh...]
where the time goes in v3:
time: 39.3 us; the launch traced here: 39.1 us
  Pallas kernels  38.5 us (98%)
  between operations  0.64 us (2%)
    pallas_call x1, Pallas kernels, shards(): pl.pallas_call(functools.partial(gather_kernel, sizes), out_shape=(jax.Sh...  33.5 us
    pallas_call x1, Pallas kernels, shards(): pl.pallas_call(functools.partial(basis_kernel, sizes), out_shape=(jax.Sha...  4.98 us

profile of v3, /device:TPU:0, one launch (start us, length us, event | category | flops | bytes accessed | tf_op | source)
XLA Modules:
  0.0 39.1 jit_solution(872170415223014514)
XLA Ops:
  0.6 33.5 %smooth_and_sum.1 = (bf16[64,240]{1,0:T(8,128)(2,1)S(1)}, f32[64,16]{1,0:T(8,128)S(1)}, bf16[160,16384]{1,0:T(8,128)(2,1)S(1)}) custom-call(f32[1024,128]{1,0:T(8,128)} %bitcast.5, f32[8192,128]{1,0:T(8,128)} %bitcast.4), custom_call_target="tpu_custom_call" | custom-call | tf_op jit(solution)/shard_map/smooth_and_sum/pallas_call | solution.py:487
  34.2 5.0 %update_basis.1 = (f32[64,128,128]{2,1,0:T(8,128)}, f32[8,64]{1,0:T(8,128)}) custom-call(bf16[64,240]{1,0:T(8,128)(2,1)S(1)} %get-tuple-element.7.weight_ref, f32[64,16]{1,0:T(8,128)S(1)} %get-tuple-element.8.coeff_ref, bf16[160,16384]{1,0:T(8,128)(2,1)S(1)} %get-tuple-element.9.z), custom_call_target="tpu_custom_call" | custom-call | tf_op jit(solution)/shard_map/update_basis/pallas_call | solution.py:532

commit v4 on v3

--- a/solution.py
+++ b/solution.py
@@ -54,19 +54,21 @@
     )
 
 
-def update_weights(sums, eofs, all_snaps, total_cells):
+def update_weights(basis_gram, snap_sums, eofs, all_snaps, total_cells):
     inv_root = 1.0 / math.sqrt(total_cells)
-    coeffs = sums[:, eofs : eofs + all_snaps] * inv_root
-    snap_gram = sums[0:all_snaps, eofs + all_snaps : eofs + 2 * all_snaps]
-    inner = (2.0 * STEP_SIZE * inv_root) * coeffs + exact(
-        coeffs, snap_gram * (STEP_SIZE * STEP_SIZE / total_cells)
-    )
-    gram = sums[:, 0:eofs] * (1.0 / total_cells) + exact(inner, coeffs, CONTRACT_LAST)
-
-    block = 8
     row = lax.broadcasted_iota(jnp.int32, (eofs, eofs), 0)
     column = lax.broadcasted_iota(jnp.int32, (eofs, eofs), 1)
-    rest = jnp.concatenate([gram, jnp.where(row == column, 1.0, 0.0)], axis=1)
+    identity = jnp.where(row == column, 1.0, 0.0)
+    coeffs_t = snap_sums[:, 0:eofs] * inv_root
+    snap_gram = snap_sums[:, eofs : eofs + all_snaps]
+    inner_t = (2.0 * STEP_SIZE * inv_root) * coeffs_t + exact(
+        snap_gram * (STEP_SIZE * STEP_SIZE / total_cells), coeffs_t
+    )
+    coeffs = exact(identity, coeffs_t, CONTRACT_LAST)
+    gram = basis_gram * (1.0 / total_cells) + exact(coeffs, inner_t)
+
+    block = 8
+    rest = jnp.concatenate([gram, identity], axis=1)
     done = []
     for first in range(0, eofs, block):
         place = lax.broadcasted_iota(jnp.int32, rest.shape, 0)
@@ -86,13 +88,14 @@
     inverse = jnp.concatenate(done, axis=0)[:, eofs : 2 * eofs]
     mix = jnp.concatenate([inverse, STEP_SIZE * exact(inverse, coeffs)], axis=1)
     high = mix.astype(jnp.bfloat16).astype(jnp.float32)
-    return coeffs, jnp.concatenate([high, high, mix - high], axis=1).astype(jnp.bfloat16)
+    return coeffs_t, jnp.concatenate([high, high, mix - high], axis=1).astype(jnp.bfloat16)
 
 
 def gather_kernel(
     sizes, snap_hbm, q_hbm, weight_ref, coeff_ref, z,
-    snap_ref, q_v, xm, xh, xs, pack, pack_in, corner, corner_in, sa, ra, rb, rc,
+    snap_ref, q_v, xm, xh, xs, pack, pack_in, corner, corner_in, sa, ra, rb, rc, late, later,
     q_sem, x_sem, halo_send, halo_recv, tm_send, tm_recv, a_send, a_recv, b_send, b_recv, c_send, c_recv,
+    d_send, d_recv, e_send, e_recv,
 ):
     snaps, levels, rows, lanes, eofs, n_lon, n_lat, n_tm = sizes
     lon, lat, tm = lax.axis_index("lon"), lax.axis_index("lat"), lax.axis_index("tm")
@@ -245,14 +248,16 @@
 
     def basis_products(step, total):
         for level in range(run):
-            part = place_basis(tm, step * run + level)
+            index = step * run + level
+            part = place_basis(index // levels, lax.rem(index, levels))
             total = total + lax.dot_general(
                 part, part, CONTRACT_LAST, preferred_element_type=jnp.float32
             )
         return total
 
+    steps = n_tm * levels // run
     qq = lax.fori_loop(
-        0, levels // run, basis_products, jnp.zeros((2 * eofs, 2 * eofs), jnp.float32)
+        0, steps // 2, basis_products, jnp.zeros((2 * eofs, 2 * eofs), jnp.float32)
     )
 
     to_left.wait()
@@ -316,7 +321,7 @@
         return carry
 
     lax.fori_loop(0, snaps, smooth, 0)
-    early, middle = snaps // 4, (5 * snaps) // 8
+    early = snaps // 4
 
     def share_rest(begin, end):
         for s in range(begin, end):
@@ -324,52 +329,62 @@
 
     share_rest(0, early)
 
-    def place_rest(step, carry):
-        for level in range(run):
-            place_basis(other, step * run + level)
-        return carry
-
-    lax.fori_loop(0, levels // run, place_rest, 0)
-
-    for s in range(snaps):
-        arrival(s, tm, s).wait_recv()
-
-    qx = jnp.zeros((2 * joint, 2 * all_snaps), jnp.float32)
-    for level in range(levels):
-        part = place_snaps(tm, level)
-        both = z[:, columns(tm, level)]
-        qx = qx + lax.dot_general(both, part, CONTRACT_LAST, preferred_element_type=jnp.float32)
+    qq = lax.fori_loop(steps // 2, steps, basis_products, qq)
 
     def fold(rows_of, count, width):
         added = rows_of[:count] + rows_of[count:]
         return added[:, :width] + added[:, width:]
 
     basis_gram = fold(qq, eofs, eofs)
-    with_snaps = fold(qx, joint, all_snaps)
-    project, snap_gram = with_snaps[:eofs], with_snaps[eofs:]
-    snap_gram = jnp.concatenate(
-        [snap_gram, jnp.zeros((eofs - all_snaps, all_snaps), jnp.float32)], axis=0
-    )
-    fill = jnp.zeros((eofs, lanes - eofs - 2 * all_snaps), jnp.float32)
-    payload = jnp.concatenate([basis_gram, project, snap_gram, fill], axis=1)
-
-    share_rows = eofs // group
+    basis_gram = jnp.concatenate(
+        [basis_gram, jnp.zeros((eofs, lanes - eofs), jnp.float32)], axis=1
+    )
+    share_rows = eofs // n_lon
     tile = sa.shape[1]
-    for g in range(group):
-        piece = payload[g * share_rows : (g + 1) * share_rows]
+    for g in range(n_lon):
+        piece = basis_gram[g * share_rows : (g + 1) * share_rows]
         if share_rows < tile:
             piece = jnp.concatenate(
                 [piece, jnp.zeros((tile - share_rows, lanes), jnp.float32)], axis=0
             )
         sa[g] = piece
     a_copies = []
-    for distance in range(1, group):
-        index, to_lon, to_tm = peer_of(distance)
-        copy = remote(sa.at[index], ra.at[distance], a_send, a_recv, distance, (to_lon, lat, to_tm))
+    for distance in range(1, n_lon):
+        to_lon = lax.rem(lon + distance, n_lon)
+        copy = remote(sa.at[to_lon], ra.at[distance], a_send, a_recv, distance, (to_lon, lat, tm))
         copy.start()
         a_copies.append(copy)
-    partial = sa[me]
-    for distance in range(1, group):
+
+    def own_products(part, level):
+        highs, lows = [], []
+        for r in range(half):
+            start = tm * (snaps * cells) + (part * half + r) * levels + level
+            field = xs[pl.ds(start, snaps, stride=cells), :]
+            high = field.astype(jnp.bfloat16).astype(jnp.float32)
+            highs.append(high)
+            lows.append(field - high)
+        mine = jnp.concatenate(
+            [jnp.concatenate(highs, axis=1), jnp.concatenate(lows, axis=1)], axis=0
+        ).astype(jnp.bfloat16)
+        where = columns(part, level)
+        both = jnp.concatenate([z[0:eofs, where], z[joint : joint + eofs, where], mine], axis=0)
+        return lax.dot_general(mine, both, CONTRACT_LAST, preferred_element_type=jnp.float32)
+
+    def own_run(step, total):
+        for level in range(run):
+            index = step * run + level
+            total = total + own_products(index // levels, lax.rem(index, levels))
+        return total
+
+    with_own = lax.fori_loop(
+        0, steps, own_run, jnp.zeros((2 * snaps, 2 * eofs + 2 * snaps), jnp.float32)
+    )
+    with_own = with_own[:snaps] + with_own[snaps:]
+    project = with_own[:, :eofs] + with_own[:, eofs : 2 * eofs]
+    own_gram = with_own[:, 2 * eofs : 2 * eofs + snaps] + with_own[:, 2 * eofs + snaps :]
+
+    partial = sa[lon]
+    for distance in range(1, n_lon):
         a_copies[distance - 1].wait_recv()
         partial = partial + ra[distance]
     rb[lat] = partial
@@ -379,7 +394,31 @@
         copy = remote(rb.at[lat], rb.at[lat], b_send, b_recv, distance, (lon, to_lat, tm))
         copy.start()
         b_copies.append(copy)
-    share_rest(early, middle)
+
+    for s in range(snaps):
+        arrival(s, tm, s).wait_recv()
+    xx = jnp.zeros((2 * all_snaps, 2 * all_snaps), jnp.float32)
+    for level in range(levels):
+        part = place_snaps(tm, level)
+        xx = xx + lax.dot_general(part, part, CONTRACT_LAST, preferred_element_type=jnp.float32)
+    row_tm = lax.broadcasted_iota(jnp.int32, (all_snaps, all_snaps), 0) // snaps
+    column_tm = lax.broadcasted_iota(jnp.int32, (all_snaps, all_snaps), 1) // snaps
+    cross = jnp.where(row_tm == column_tm, 0.0, fold(xx, all_snaps, all_snaps))
+    own_gram = jnp.concatenate([jnp.concatenate([own_gram] * n_tm, axis=1)] * n_tm, axis=0)
+    snap_gram = jnp.where((row_tm == tm) & (column_tm == tm), own_gram, cross)
+    project = jnp.concatenate([project] * n_tm, axis=0)
+    owner = lax.broadcasted_iota(jnp.int32, (all_snaps, eofs), 0) // snaps
+    project = jnp.where(owner == tm, project, 0.0)
+    fill = jnp.zeros((all_snaps, lanes - eofs - all_snaps), jnp.float32)
+    late[me] = jnp.concatenate([project, snap_gram, fill], axis=1)
+    d_copies = []
+    for distance in range(1, group):
+        _, to_lon, to_tm = peer_of(distance)
+        copy = remote(late.at[me], late.at[me], d_send, d_recv, distance, (to_lon, lat, to_tm))
+        copy.start()
+        d_copies.append(copy)
+    share_rest(early, snaps)
+
     for distance in range(1, n_lat):
         from_lat = lax.rem(lat + n_lat - distance, n_lat)
         remote(rb.at[from_lat], rb.at[from_lat], b_send, b_recv, distance, (lon, from_lat, tm)).wait_recv()
@@ -388,20 +427,46 @@
     summed = rb[0]
     for index in range(1, n_lat):
         summed = summed + rb[index]
-    rc[me] = summed
+    rc[lon] = summed
     c_copies = []
-    for distance in range(1, group):
-        _, to_lon, to_tm = peer_of(distance)
-        copy = remote(rc.at[me], rc.at[me], c_send, c_recv, distance, (to_lon, lat, to_tm))
+    for distance in range(1, n_lon):
+        to_lon = lax.rem(lon + distance, n_lon)
+        copy = remote(rc.at[lon], rc.at[lon], c_send, c_recv, distance, (to_lon, lat, tm))
         copy.start()
         c_copies.append(copy)
-    share_rest(middle, snaps)
+
     for distance in range(1, group):
-        source = lax.rem(me + group - distance, group)
-        remote(rc.at[source], rc.at[source], c_send, c_recv, distance, (lon, lat, other)).wait_recv()
-    sums = jnp.concatenate([rc[g, 0:share_rows] for g in range(group)], axis=0)
-    coeffs, weights = update_weights(sums, eofs, all_snaps, cells * lanes * n_lon * n_lat)
-    coeff_ref[...] = coeffs
+        source, from_lon, from_tm = peer_of(group - distance)
+        remote(late.at[source], late.at[source], d_send, d_recv, distance, (from_lon, lat, from_tm)).wait_recv()
+    for copy in d_copies:
+        copy.wait_send()
+    summed = late[0]
+    for index in range(1, group):
+        summed = summed + late[index]
+    later[lat] = summed
+    e_copies = []
+    for distance in range(1, n_lat):
+        to_lat = lax.rem(lat + distance, n_lat)
+        copy = remote(later.at[lat], later.at[lat], e_send, e_recv, distance, (lon, to_lat, tm))
+        copy.start()
+        e_copies.append(copy)
+
+    for distance in range(1, n_lon):
+        source = lax.rem(lon + n_lon - distance, n_lon)
+        remote(rc.at[source], rc.at[source], c_send, c_recv, distance, (source, lat, tm)).wait_recv()
+    basis_gram = jnp.concatenate([rc[g, 0:share_rows] for g in range(n_lon)], axis=0)[:, 0:eofs]
+    for distance in range(1, n_lat):
+        from_lat = lax.rem(lat + n_lat - distance, n_lat)
+        remote(later.at[from_lat], later.at[from_lat], e_send, e_recv, distance, (lon, from_lat, tm)).wait_recv()
+    for copy in e_copies:
+        copy.wait_send()
+    snap_sums = later[0]
+    for index in range(1, n_lat):
+        snap_sums = snap_sums + later[index]
+    coeffs_t, weights = update_weights(
+        basis_gram, snap_sums, eofs, all_snaps, cells * lanes * n_lon * n_lat
+    )
+    coeff_ref[...] = coeffs_t
     weight_ref[...] = weights
 
     for s in range(snaps):
@@ -461,9 +526,7 @@
         return carry
 
     lax.fori_loop(0, n_tm * levels // run, one_run, 0)
-    chosen = lax.broadcasted_iota(jnp.int32, (snaps, all_snaps), 0) + lax.axis_index("tm") * snaps
-    column = lax.broadcasted_iota(jnp.int32, (snaps, all_snaps), 1)
-    own_ref[...] = exact(jnp.where(chosen == column, 1.0, 0.0), coeff_ref[...], CONTRACT_LAST)
+    own_ref[...] = coeff_ref[pl.ds(pl.multiple_of(lax.axis_index("tm") * snaps, snaps), snaps), :]
     for step in range(n_tm * levels):
         block(step).wait()
 
@@ -477,7 +540,7 @@
     group = n_lon * n_tm
     all_snaps = n_tm * snaps
     joint = eofs + all_snaps
-    tile = max(8, eofs // group)
+    tile = max(8, eofs // n_lon)
     f32, bf16 = jnp.float32, jnp.bfloat16
     dma = pltpu.SemaphoreType.DMA
     vmem = pl.BlockSpec(memory_space=pltpu.VMEM)
@@ -488,7 +551,7 @@
         functools.partial(gather_kernel, sizes),
         out_shape=(
             jax.ShapeDtypeStruct((eofs, 3 * joint), bf16),
-            jax.ShapeDtypeStruct((eofs, all_snaps), f32),
+            jax.ShapeDtypeStruct((all_snaps, eofs), f32),
             jax.ShapeDtypeStruct((2 * joint, cells * lanes), bf16),
         ),
         in_specs=[in_hbm, in_hbm],
@@ -503,22 +566,28 @@
             pltpu.VMEM((2, snaps, levels, lanes), f32),
             pltpu.VMEM((4, levels, lanes), f32),
             pltpu.VMEM((4, levels, lanes), f32),
-            pltpu.VMEM((group, tile, lanes), f32),
-            pltpu.VMEM((group, tile, lanes), f32),
+            pltpu.VMEM((n_lon, tile, lanes), f32),
+            pltpu.VMEM((n_lon, tile, lanes), f32),
             pltpu.VMEM((n_lat, tile, lanes), f32),
-            pltpu.VMEM((group, tile, lanes), f32),
+            pltpu.VMEM((n_lon, tile, lanes), f32),
+            pltpu.VMEM((group, all_snaps, lanes), f32),
+            pltpu.VMEM((n_lat, all_snaps, lanes), f32),
             dma,
             dma,
             dma((8,)),
             dma((8,)),
             dma((2 * snaps,)),
             dma((2 * snaps,)),
+            dma((n_lon,)),
+            dma((n_lon,)),
+            dma((n_lat,)),
+            dma((n_lat,)),
+            dma((n_lon,)),
+            dma((n_lon,)),
             dma((group,)),
             dma((group,)),
             dma((n_lat,)),
             dma((n_lat,)),
-            dma((group,)),
-            dma((group,)),
         ],
         compiler_params=pltpu.CompilerParams(
             collective_id=0, has_side_effects=True, vmem_limit_bytes=40 * 2**20

time: 39.3 us -> 35.8 us (0.911)
  Pallas kernels: 38.5 us -> 35 us
    pallas_call x1, Pallas kernels: 33.5 us -> 30 us  [shards(): pl.pallas_call(functools.partial(gather_kernel, sizes), out_shape=(jax.Sh...]
where the time goes in v4:
time: 35.8 us; the launch traced here: 35.6 us
  Pallas kernels  35 us (98%)
  between operations  0.64 us (2%)
    pallas_call x1, Pallas kernels, shards(): pl.pallas_call(functools.partial(gather_kernel, sizes), out_shape=(jax.Sh...  30 us
    pallas_call x1, Pallas kernels, shards(): pl.pallas_call(functools.partial(basis_kernel, sizes), out_shape=(jax.Sha...  4.98 us

profile of v4, /device:TPU:0, one launch (start us, length us, event | category | flops | bytes accessed | tf_op | source)
XLA Modules:
  0.0 35.6 jit_solution(9666645568558322776)
XLA Ops:
  0.6 30.0 %smooth_and_sum.1 = (bf16[64,240]{1,0:T(8,128)(2,1)S(1)}, f32[16,64]{1,0:T(8,128)S(1)}, bf16[160,16384]{1,0:T(8,128)(2,1)S(1)}) custom-call(f32[1024,128]{1,0:T(8,128)} %bitcast.5, f32[8192,128]{1,0:T(8,128)} %bitcast.4), custom_call_target="tpu_custom_call" | custom-call | tf_op jit(solution)/shard_map/smooth_and_sum/pallas_call | solution.py:550
  30.6 5.0 %update_basis.1 = (f32[64,128,128]{2,1,0:T(8,128)}, f32[8,64]{1,0:T(8,128)}) custom-call(bf16[64,240]{1,0:T(8,128)(2,1)S(1)} %get-tuple-element.7.weight_ref, f32[16,64]{1,0:T(8,128)S(1)} %get-tuple-element.8.coeff_ref, bf16[160,16384]{1,0:T(8,128)(2,1)S(1)} %get-tuple-element.9.z), custom_call_target="tpu_custom_call" | custom-call | tf_op jit(solution)/shard_map/update_basis/pallas_call | solution.py:601

commit v5 on v4

--- a/solution.py
+++ b/solution.py
@@ -24,6 +24,10 @@
     return lax.dot_general(
         left, right, dims, precision=lax.Precision.HIGHEST, preferred_element_type=jnp.float32
     )
+
+
+def pitch_of(cells):
+    return cells + 8 * (1 - cells // 8 % 2)
 
 
 def smooth_rows(main, halo):
@@ -106,10 +110,12 @@
     has_up, has_down = lat > 0, lat < n_lat - 1
     cells = rows * levels
     half = rows // n_tm
+    pitch = pitch_of(cells)
+    q_rows = q_v.reshape(eofs * pitch, lanes)
 
     snap_copy = pltpu.make_async_copy(snap_hbm, snap_ref, x_sem)
     snap_copy.start()
-    q_copy = pltpu.make_async_copy(q_hbm, q_v, q_sem)
+    q_copy = pltpu.make_async_copy(q_hbm, q_v.at[:, pl.ds(0, cells), :], q_sem)
     q_copy.start()
 
     barrier = pltpu.get_barrier_semaphore()
@@ -227,13 +233,13 @@
     def split_rows(ref, count, start, step):
         highs, lows = [], []
         for r in range(half):
-            high, low = split(ref[pl.ds(start + r * step, count, stride=cells), :])
+            high, low = split(ref[pl.ds(start + r * step, count, stride=pitch), :])
             highs.append(high)
             lows.append(low)
         return jnp.concatenate(highs, axis=1), jnp.concatenate(lows, axis=1)
 
     def place_basis(part, level):
-        high, low = split_rows(q_v, eofs, level * rows + part * half, 1)
+        high, low = split_rows(q_rows, eofs, level * rows + part * half, 1)
         z[0:eofs, columns(part, level)] = high
         z[joint : joint + eofs, columns(part, level)] = low
         return jnp.concatenate([high, low], axis=0)
@@ -298,12 +304,12 @@
     down_flag = has_down.astype(jnp.float32)
 
     def share(s, part, slot):
-        begin = pl.multiple_of(tm * (snaps * cells) + s * cells + part * (half * levels), levels)
+        begin = pl.multiple_of(tm * (snaps * pitch) + s * pitch + part * (half * levels), levels)
         where = pl.ds(begin, half * levels)
         return remote(xs.at[where], xs.at[where], tm_send, tm_recv, slot, (lon, lat, other))
 
     def arrival(s, part, slot):
-        begin = pl.multiple_of(other * (snaps * cells) + s * cells + part * (half * levels), levels)
+        begin = pl.multiple_of(other * (snaps * pitch) + s * pitch + part * (half * levels), levels)
         where = pl.ds(begin, half * levels)
         return remote(xs.at[where], xs.at[where], tm_send, tm_recv, slot, (lon, lat, other))
 
@@ -315,7 +321,7 @@
             main, halo = smooth_rows(main, halo)
             main = edge_masked(main, W - 1 - sweep, up_flag, down_flag)
             halo = edge_masked(halo, W - 1 - sweep, up_flag, down_flag)
-        begin = pl.multiple_of(tm * (snaps * cells) + s * cells, cells)
+        begin = pl.multiple_of(tm * (snaps * pitch) + s * pitch, levels)
         xs[pl.ds(begin, cells), :] = main.reshape(cells, lanes)
         share(s, other, s).start()
         return carry
@@ -358,8 +364,8 @@
     def own_products(part, level):
         highs, lows = [], []
         for r in range(half):
-            start = tm * (snaps * cells) + (part * half + r) * levels + level
-            field = xs[pl.ds(start, snaps, stride=cells), :]
+            start = tm * (snaps * pitch) + (part * half + r) * levels + level
+            field = xs[pl.ds(start, snaps, stride=pitch), :]
             high = field.astype(jnp.bfloat16).astype(jnp.float32)
             highs.append(high)
             lows.append(field - high)
@@ -500,7 +506,8 @@
     cells = rows * levels
     half = rows // n_tm
     wide = half * lanes
-    out_rows = o_v.reshape(eofs * cells, lanes)
+    pitch = pitch_of(cells)
+    out_rows = o_v.reshape(eofs * pitch, lanes)
     weights = weight_ref[...]
 
     def block(step):
@@ -520,8 +527,8 @@
                 stack = jnp.concatenate([z[:, where], z[0:joint, where]], axis=0)
                 result = jnp.dot(weights, stack, preferred_element_type=jnp.float32)
                 start = level * rows + part * half + r
-                out_rows[pl.ds(start, eofs, stride=cells), :] = result[:, :lanes]
-                out_rows[pl.ds(start + 1, eofs, stride=cells), :] = result[:, lanes:]
+                out_rows[pl.ds(start, eofs, stride=pitch), :] = result[:, :lanes]
+                out_rows[pl.ds(start + 1, eofs, stride=pitch), :] = result[:, lanes:]
             block(step).start()
         return carry
 
@@ -545,7 +552,8 @@
     dma = pltpu.SemaphoreType.DMA
     vmem = pl.BlockSpec(memory_space=pltpu.VMEM)
     in_hbm = pl.BlockSpec(memory_space=pltpu.HBM)
-    flat = basis.reshape(eofs * cells, lanes)
+    flat = basis.reshape(eofs, cells, lanes)
+    pitch = pitch_of(cells)
 
     weights, coeffs, parts = pl.pallas_call(
         functools.partial(gather_kernel, sizes),
@@ -558,10 +566,10 @@
         out_specs=(vmem, vmem, vmem),
         scratch_shapes=[
             pltpu.VMEM((snaps * cells, lanes), f32),
-            pltpu.VMEM((eofs * cells, lanes), f32),
+            pltpu.VMEM((eofs, pitch, lanes), f32),
             pltpu.VMEM((snaps, rows + 2 * W, levels, lanes), f32),
             pltpu.VMEM((snaps, rows + 2 * W, levels, lanes), f32),
-            pltpu.VMEM((all_snaps * cells, lanes), f32),
+            pltpu.VMEM((all_snaps * pitch, lanes), f32),
             pltpu.VMEM((2, snaps, levels, lanes), f32),
             pltpu.VMEM((2, snaps, levels, lanes), f32),
             pltpu.VMEM((4, levels, lanes), f32),
@@ -607,7 +615,7 @@
         in_specs=[vmem, vmem, vmem],
         out_specs=(in_hbm, vmem),
         scratch_shapes=[
-            pltpu.VMEM((eofs, cells, lanes), f32),
+            pltpu.VMEM((eofs, pitch, lanes), f32),
             dma((n_tm * levels,)),
         ],
         compiler_params=pltpu.CompilerParams(vmem_limit_bytes=32 * 2**20),

time: 35.8 us -> 33.8 us (0.944)
  Pallas kernels: 35 us -> 33 us
    pallas_call x1, Pallas kernels: 4.98 us -> 3.25 us  [shards(): pl.pallas_call(functools.partial(basis_kernel, sizes), out_shape=(jax.Sha...]
where the time goes in v5:
time: 33.8 us; the launch traced here: 33.7 us
  Pallas kernels  33 us (98%)
  between operations  0.64 us (2%)
    pallas_call x1, Pallas kernels, shards(): pl.pallas_call(functools.partial(gather_kernel, sizes), out_shape=(jax.Sh...  29.8 us
    pallas_call x1, Pallas kernels, shards(): pl.pallas_call(functools.partial(basis_kernel, sizes), out_shape=(jax.Sha...  3.25 us

profile of v5, /device:TPU:0, one launch (start us, length us, event | category | flops | bytes accessed | tf_op | source)
XLA Modules:
  0.0 33.7 jit_solution(4167031917786793680)
XLA Ops:
  0.6 29.8 %smooth_and_sum.1 = (bf16[64,240]{1,0:T(8,128)(2,1)S(1)}, f32[16,64]{1,0:T(8,128)S(1)}, bf16[160,16384]{1,0:T(8,128)(2,1)S(1)}) custom-call(f32[1024,128]{1,0:T(8,128)} %bitcast.5, f32[64,128,128]{2,1,0:T(8,128)} %bitcast.4), custom_call_target="tpu_custom_call" | custom-call | tf_op jit(solution)/shard_map/smooth_and_sum/pallas_call | solution.py:558
  30.4 3.2 %update_basis.1 = (f32[64,128,128]{2,1,0:T(8,128)}, f32[8,64]{1,0:T(8,128)}) custom-call(bf16[64,240]{1,0:T(8,128)(2,1)S(1)} %get-tuple-element.7.weight_ref, f32[16,64]{1,0:T(8,128)S(1)} %get-tuple-element.8.coeff_ref, bf16[160,16384]{1,0:T(8,128)(2,1)S(1)} %get-tuple-element.9.z), custom_call_target="tpu_custom_call" | custom-call | tf_op jit(solution)/shard_map/update_basis/pallas_call | solution.py:609

commit v6 on v5

--- a/solution.py
+++ b/solution.py
@@ -73,22 +73,40 @@
 
     block = 8
     rest = jnp.concatenate([gram, identity], axis=1)
+    width = 2 * eofs
+    sub = lax.broadcasted_iota(jnp.int32, (block, width), 0)
     done = []
     for first in range(0, eofs, block):
-        place = lax.broadcasted_iota(jnp.int32, rest.shape, 0)
         spread = [
             jnp.broadcast_to(rest[:, first + i : first + i + 1], rest.shape) for i in range(block)
         ]
-        pivots = jnp.ones((block, rest.shape[1]), jnp.float32)
+        head = [
+            [jnp.broadcast_to(spread[n][m : m + 1, :], (block, width)) for n in range(m + 1)]
+            for m in range(block)
+        ]
+        lines = [jnp.broadcast_to(rest[m : m + 1, :], (block, width)) for m in range(block)]
+        more = rest.shape[0] > block
+        if more:
+            below = rest[block:].reshape(-1, block, width)
+            sides = [part[block:].reshape(-1, block, width) for part in spread]
         for i in range(block):
-            pivot = spread[i][i : i + 1, :]
-            pivots = jnp.where(place[:block] == i, pivot, pivots)
-            factor = jnp.where(place > i, spread[i], 0.0) * (1.0 / pivot)
-            for n in range(i + 1, block):
-                spread[n] = spread[n] - factor * spread[i][n : n + 1, :]
-            rest = rest - factor * rest[i : i + 1, :]
-        done.append(rest[:block] * (1.0 / jnp.sqrt(pivots)))
-        rest = rest[block:]
+            inverse_pivot = 1.0 / head[i][i]
+            for m in range(i + 1, block):
+                factor = head[m][i] * inverse_pivot
+                for n in range(i + 1, m + 1):
+                    head[m][n] = head[m][n] - factor * head[n][i]
+                lines[m] = lines[m] - factor * lines[i]
+            if more:
+                factor = sides[i] * inverse_pivot
+                for n in range(i + 1, block):
+                    sides[n] = sides[n] - factor * head[n][i]
+                below = below - factor * lines[i]
+        finished = jnp.zeros((block, width), jnp.float32)
+        for i in range(block):
+            finished = jnp.where(sub == i, lines[i] * (1.0 / jnp.sqrt(head[i][i])), finished)
+        done.append(finished)
+        if more:
+            rest = below.reshape(-1, width)
     inverse = jnp.concatenate(done, axis=0)[:, eofs : 2 * eofs]
     mix = jnp.concatenate([inverse, STEP_SIZE * exact(inverse, coeffs)], axis=1)
     high = mix.astype(jnp.bfloat16).astype(jnp.float32)
@@ -327,13 +345,6 @@
         return carry
 
     lax.fori_loop(0, snaps, smooth, 0)
-    early = snaps // 4
-
-    def share_rest(begin, end):
-        for s in range(begin, end):
-            share(s, tm, snaps + s).start()
-
-    share_rest(0, early)
 
     qq = lax.fori_loop(steps // 2, steps, basis_products, qq)
 
@@ -423,7 +434,8 @@
         copy = remote(late.at[me], late.at[me], d_send, d_recv, distance, (to_lon, lat, to_tm))
         copy.start()
         d_copies.append(copy)
-    share_rest(early, snaps)
+    for s in range(snaps):
+        share(s, tm, snaps + s).start()
 
     for distance in range(1, n_lat):
         from_lat = lax.rem(lat + n_lat - distance, n_lat)

time: 33.8 us -> 33.5 us (level)
  no operation moved by 1% of the time
where the time goes in v6:
time: 33.5 us; the launch traced here: 33.4 us
  Pallas kernels  32.7 us (98%)
  between operations  0.64 us (2%)
    pallas_call x1, Pallas kernels, shards(): pl.pallas_call(functools.partial(gather_kernel, sizes), out_shape=(jax.Sh...  29.5 us
    pallas_call x1, Pallas kernels, shards(): pl.pallas_call(functools.partial(basis_kernel, sizes), out_shape=(jax.Sha...  3.24 us

profile of v6, /device:TPU:0, one launch (start us, length us, event | category | flops | bytes accessed | tf_op | source)
XLA Modules:
  0.0 33.4 jit_solution(7915991448068529013)
XLA Ops:
  0.6 29.5 %smooth_and_sum.1 = (bf16[64,240]{1,0:T(8,128)(2,1)S(1)}, f32[16,64]{1,0:T(8,128)S(1)}, bf16[160,16384]{1,0:T(8,128)(2,1)S(1)}) custom-call(f32[1024,128]{1,0:T(8,128)} %bitcast.5, f32[64,128,128]{2,1,0:T(8,128)} %bitcast.4), custom_call_target="tpu_custom_call" | custom-call | tf_op jit(solution)/shard_map/smooth_and_sum/pallas_call | solution.py:570
  30.1 3.2 %update_basis.1 = (f32[64,128,128]{2,1,0:T(8,128)}, f32[8,64]{1,0:T(8,128)}) custom-call(bf16[64,240]{1,0:T(8,128)(2,1)S(1)} %get-tuple-element.7.weight_ref, f32[16,64]{1,0:T(8,128)S(1)} %get-tuple-element.8.coeff_ref, bf16[160,16384]{1,0:T(8,128)(2,1)S(1)} %get-tuple-element.9.z), custom_call_target="tpu_custom_call" | custom-call | tf_op jit(solution)/shard_map/update_basis/pallas_call | solution.py:621

commit v7 on v6

--- a/solution.py
+++ b/solution.py
@@ -345,6 +345,9 @@
         return carry
 
     lax.fori_loop(0, snaps, smooth, 0)
+    early = snaps // 4
+    for s in range(early):
+        share(s, tm, snaps + s).start()
 
     qq = lax.fori_loop(steps // 2, steps, basis_products, qq)
 
@@ -434,7 +437,7 @@
         copy = remote(late.at[me], late.at[me], d_send, d_recv, distance, (to_lon, lat, to_tm))
         copy.start()
         d_copies.append(copy)
-    for s in range(snaps):
+    for s in range(early, snaps):
         share(s, tm, snaps + s).start()
 
     for distance in range(1, n_lat):
@@ -527,7 +530,7 @@
         where = pl.ds(pl.multiple_of(level * rows + part * half, half), half)
         return pltpu.make_async_copy(o_v.at[:, where, :], out_hbm.at[:, where, :], o_sem.at[step])
 
-    run = 4 if levels % 4 == 0 else 1
+    run = levels
 
     def one_run(index, carry):
         for inner in range(run):

time: 33.5 us -> 33.9 us (1.012)
  Pallas kernels: 32.7 us -> 33.1 us
    pallas_call x1, Pallas kernels: 29.5 us -> 30 us  [shards(): pl.pallas_call(functools.partial(gather_kernel, sizes), out_shape=(jax.Sh...]
where the time goes in v7:
time: 33.9 us; the launch traced here: 33.8 us
  Pallas kernels  33.1 us (98%)
  between operations  0.64 us (2%)
    pallas_call x1, Pallas kernels, shards(): pl.pallas_call(functools.partial(gather_kernel, sizes), out_shape=(jax.Sh...  30 us
    pallas_call x1, Pallas kernels, shards(): pl.pallas_call(functools.partial(basis_kernel, sizes), out_shape=(jax.Sha...  3.18 us

profile of v7, /device:TPU:0, one launch (start us, length us, event | category | flops | bytes accessed | tf_op | source)
XLA Modules:
  0.0 33.8 jit_solution(12520313949097216101)
XLA Ops:
  0.6 30.0 %smooth_and_sum.1 = (bf16[64,240]{1,0:T(8,128)(2,1)S(1)}, f32[16,64]{1,0:T(8,128)S(1)}, bf16[160,16384]{1,0:T(8,128)(2,1)S(1)}) custom-call(f32[1024,128]{1,0:T(8,128)} %bitcast.5, f32[64,128,128]{2,1,0:T(8,128)} %bitcast.4), custom_call_target="tpu_custom_call" | custom-call | tf_op jit(solution)/shard_map/smooth_and_sum/pallas_call | solution.py:573
  30.6 3.2 %update_basis.1 = (f32[64,128,128]{2,1,0:T(8,128)}, f32[8,64]{1,0:T(8,128)}) custom-call(bf16[64,240]{1,0:T(8,128)(2,1)S(1)} %get-tuple-element.7.weight_ref, f32[16,64]{1,0:T(8,128)S(1)} %get-tuple-element.8.coeff_ref, bf16[160,16384]{1,0:T(8,128)(2,1)S(1)} %get-tuple-element.9.z), custom_call_target="tpu_custom_call" | custom-call | tf_op jit(solution)/shard_map/update_basis/pallas_call | solution.py:624

commit v8 on v6

--- a/solution.py
+++ b/solution.py
@@ -281,72 +281,8 @@
 
     steps = n_tm * levels // run
     qq = lax.fori_loop(
-        0, steps // 2, basis_products, jnp.zeros((2 * eofs, 2 * eofs), jnp.float32)
-    )
-
-    to_left.wait()
-    to_right.wait()
-
-    @pl.when(has_down)
-    def _():
-        up_in = [
-            remote(xm.at[:, pl.ds(W, W)], xm.at[:, pl.ds(W + rows, W)], halo_send, halo_recv, 2, (lon, lat, tm)),
-            remote(corner.at[0], corner_in.at[0], halo_send, halo_recv, 3, (lon, lat, tm)),
-            remote(corner.at[1], corner_in.at[1], halo_send, halo_recv, 4, (lon, lat, tm)),
-        ]
-        for copy in up_in:
-            copy.wait_recv()
-
-    @pl.when(has_up)
-    def _():
-        down_in = [
-            remote(xm.at[:, pl.ds(rows, W)], xm.at[:, pl.ds(0, W)], halo_send, halo_recv, 5, (lon, lat, tm)),
-            remote(corner.at[2], corner_in.at[2], halo_send, halo_recv, 6, (lon, lat, tm)),
-            remote(corner.at[3], corner_in.at[3], halo_send, halo_recv, 7, (lon, lat, tm)),
-        ]
-        for copy in down_in:
-            copy.wait_recv()
-
-    def beside(from_right, from_left, offset):
-        low = from_right if offset == 0 else pltpu.roll(from_right, (lanes - offset) % lanes, 1)
-        high = pltpu.roll(from_left, (lanes - W - offset) % lanes, 1)
-        return jnp.where(lane < W, low, jnp.where(lane >= lanes - W, high, 0.0))
-
-    for s in range(snaps):
-        for j in range(W):
-            offset = span * s + W * j
-            xh[s, j] = beside(corner_in[2], corner_in[3], offset)
-            xh[s, W + rows + j] = beside(corner_in[0], corner_in[1], offset)
-
-    up_flag = has_up.astype(jnp.float32)
-    down_flag = has_down.astype(jnp.float32)
-
-    def share(s, part, slot):
-        begin = pl.multiple_of(tm * (snaps * pitch) + s * pitch + part * (half * levels), levels)
-        where = pl.ds(begin, half * levels)
-        return remote(xs.at[where], xs.at[where], tm_send, tm_recv, slot, (lon, lat, other))
-
-    def arrival(s, part, slot):
-        begin = pl.multiple_of(other * (snaps * pitch) + s * pitch + part * (half * levels), levels)
-        where = pl.ds(begin, half * levels)
-        return remote(xs.at[where], xs.at[where], tm_send, tm_recv, slot, (lon, lat, other))
-
-    def smooth(s, carry):
-        for r in range(rows):
-            xh[s, W + r] = beside(pack_in[0, s], pack_in[1, s], W * r)
-        main, halo = xm[s], xh[s]
-        for sweep in range(W):
-            main, halo = smooth_rows(main, halo)
-            main = edge_masked(main, W - 1 - sweep, up_flag, down_flag)
-            halo = edge_masked(halo, W - 1 - sweep, up_flag, down_flag)
-        begin = pl.multiple_of(tm * (snaps * pitch) + s * pitch, levels)
-        xs[pl.ds(begin, cells), :] = main.reshape(cells, lanes)
-        share(s, other, s).start()
-        return carry
-
-    lax.fori_loop(0, snaps, smooth, 0)
-
-    qq = lax.fori_loop(steps // 2, steps, basis_products, qq)
+        0, steps, basis_products, jnp.zeros((2 * eofs, 2 * eofs), jnp.float32)
+    )
 
     def fold(rows_of, count, width):
         added = rows_of[:count] + rows_of[count:]
@@ -371,6 +307,68 @@
         copy = remote(sa.at[to_lon], ra.at[distance], a_send, a_recv, distance, (to_lon, lat, tm))
         copy.start()
         a_copies.append(copy)
+
+    to_left.wait()
+    to_right.wait()
+
+    @pl.when(has_down)
+    def _():
+        up_in = [
+            remote(xm.at[:, pl.ds(W, W)], xm.at[:, pl.ds(W + rows, W)], halo_send, halo_recv, 2, (lon, lat, tm)),
+            remote(corner.at[0], corner_in.at[0], halo_send, halo_recv, 3, (lon, lat, tm)),
+            remote(corner.at[1], corner_in.at[1], halo_send, halo_recv, 4, (lon, lat, tm)),
+        ]
+        for copy in up_in:
+            copy.wait_recv()
+
+    @pl.when(has_up)
+    def _():
+        down_in = [
+            remote(xm.at[:, pl.ds(rows, W)], xm.at[:, pl.ds(0, W)], halo_send, halo_recv, 5, (lon, lat, tm)),
+            remote(corner.at[2], corner_in.at[2], halo_send, halo_recv, 6, (lon, lat, tm)),
+            remote(corner.at[3], corner_in.at[3], halo_send, halo_recv, 7, (lon, lat, tm)),
+        ]
+        for copy in down_in:
+            copy.wait_recv()
+
+    def beside(from_right, from_left, offset):
+        low = from_right if offset == 0 else pltpu.roll(from_right, (lanes - offset) % lanes, 1)
+        high = pltpu.roll(from_left, (lanes - W - offset) % lanes, 1)
+        return jnp.where(lane < W, low, jnp.where(lane >= lanes - W, high, 0.0))
+
+    for s in range(snaps):
+        for j in range(W):
+            offset = span * s + W * j
+            xh[s, j] = beside(corner_in[2], corner_in[3], offset)
+            xh[s, W + rows + j] = beside(corner_in[0], corner_in[1], offset)
+
+    up_flag = has_up.astype(jnp.float32)
+    down_flag = has_down.astype(jnp.float32)
+
+    def share(s, part, slot):
+        begin = pl.multiple_of(tm * (snaps * pitch) + s * pitch + part * (half * levels), levels)
+        where = pl.ds(begin, half * levels)
+        return remote(xs.at[where], xs.at[where], tm_send, tm_recv, slot, (lon, lat, other))
+
+    def arrival(s, part, slot):
+        begin = pl.multiple_of(other * (snaps * pitch) + s * pitch + part * (half * levels), levels)
+        where = pl.ds(begin, half * levels)
+        return remote(xs.at[where], xs.at[where], tm_send, tm_recv, slot, (lon, lat, other))
+
+    def smooth(s, carry):
+        for r in range(rows):
+            xh[s, W + r] = beside(pack_in[0, s], pack_in[1, s], W * r)
+        main, halo = xm[s], xh[s]
+        for sweep in range(W):
+            main, halo = smooth_rows(main, halo)
+            main = edge_masked(main, W - 1 - sweep, up_flag, down_flag)
+            halo = edge_masked(halo, W - 1 - sweep, up_flag, down_flag)
+        begin = pl.multiple_of(tm * (snaps * pitch) + s * pitch, levels)
+        xs[pl.ds(begin, cells), :] = main.reshape(cells, lanes)
+        share(s, other, s).start()
+        return carry
+
+    lax.fori_loop(0, snaps, smooth, 0)
 
     def own_products(part, level):
         highs, lows = [], []

time: 33.5 us -> 33.5 us (level)
  no operation moved by 1% of the time
where the time goes in v8:
time: 33.5 us; the launch traced here: 33.4 us
  Pallas kernels  32.7 us (98%)
  between operations  0.64 us (2%)
    pallas_call x1, Pallas kernels, shards(): pl.pallas_call(functools.partial(gather_kernel, sizes), out_shape=(jax.Sh...  29.5 us
    pallas_call x1, Pallas kernels, shards(): pl.pallas_call(functools.partial(basis_kernel, sizes), out_shape=(jax.Sha...  3.24 us

profile of v8, /device:TPU:0, one launch (start us, length us, event | category | flops | bytes accessed | tf_op | source)
XLA Modules:
  0.0 33.4 jit_solution(12629620308175444939)
XLA Ops:
  0.6 29.5 %smooth_and_sum.1 = (bf16[64,240]{1,0:T(8,128)(2,1)S(1)}, f32[16,64]{1,0:T(8,128)S(1)}, bf16[160,16384]{1,0:T(8,128)(2,1)S(1)}) custom-call(f32[1024,128]{1,0:T(8,128)} %bitcast.5, f32[64,128,128]{2,1,0:T(8,128)} %bitcast.4), custom_call_target="tpu_custom_call" | custom-call | tf_op jit(solution)/shard_map/smooth_and_sum/pallas_call | solution.py:568
  30.1 3.2 %update_basis.1 = (f32[64,128,128]{2,1,0:T(8,128)}, f32[8,64]{1,0:T(8,128)}) custom-call(bf16[64,240]{1,0:T(8,128)(2,1)S(1)} %get-tuple-element.7.weight_ref, f32[16,64]{1,0:T(8,128)S(1)} %get-tuple-element.8.coeff_ref, bf16[160,16384]{1,0:T(8,128)(2,1)S(1)} %get-tuple-element.9.z), custom_call_target="tpu_custom_call" | custom-call | tf_op jit(solution)/shard_map/update_basis/pallas_call | solution.py:619
